TPU v7x, 32 devices: a whole 2x2x4 slice. The times are simulated.
32 devices in a mesh: dp: 4 (over y, core), mp: 8 (over z, x).
Axes of the slice: x: 2, y: 2, z: 4, core: 2. Of those that a mesh axis runs over, the one named last changes fastest.
Arguments:
- tokens: bfloat16 [16384, 1152], P(('dp', 'mp')), may hold values from -6 to 6
- conditioning: bfloat16 [64, 1152], P('dp'), may hold values from -6 to 6
- counts: int32 [4], P('dp'), may hold values from 1 to 16, as said below
- offset_index: int32 [256, 256], replicated, may hold values from 0 to 960, as said below
- modulator: bfloat16 [1152, 6912], P(None, 'mp'), may hold values from -0.1875 to 0.1875
- modulator_bias: bfloat16 [6912], P('mp'), may hold values from -3 to 3
- qkv_weight: bfloat16 [1152, 3, 1152], P(None, None, 'mp'), may hold values from -0.1875 to 0.1875
- qv_bias: bfloat16 [2, 1152], P(None, 'mp'), may hold values from -3 to 3
- offset_table: bfloat16 [961, 16], P(None, 'mp'), may hold values from -4 to 4
- out_weight: bfloat16 [1152, 1152], P('mp'), may hold values from -1 to 1
- out_bias: bfloat16 [1152], replicated, may hold values from -3 to 3
- up_weight: bfloat16 [1152, 4608], P(None, 'mp'), may hold values from -0.1875 to 0.1875
- up_bias: bfloat16 [4608], P('mp'), may hold values from -3 to 3
- down_weight: bfloat16 [4608, 1152], P('mp'), may hold values from -0.09375 to 0.09375
- down_bias: bfloat16 [1152], replicated, may hold values from -3 to 3
- out_grad: bfloat16 [16384, 1152], P(('dp', 'mp')), may hold values from -6 to 6
Outputs:
- block_out: bfloat16 [16384, 1152], P(('dp', 'mp'))
- tokens_grad: float32 [16384, 1152], P(('dp', 'mp'))
- cond_grad: float32 [64, 1152], P('dp')
- modulator_grad: float32 [1152, 6912], P(None, 'mp')
- modulator_bias_grad: float32 [6912], P('mp')
- qkv_grad: float32 [1152, 3, 1152], P(None, None, 'mp')
- qv_bias_grad: float32 [2, 1152], P(None, 'mp')
- offset_table_grad: float32 [961, 16], P(None, 'mp')
- out_weight_grad: float32 [1152, 1152], P('mp')
- out_bias_grad: float32 [1152], replicated
- up_grad: float32 [1152, 4608], P(None, 'mp')
- up_bias_grad: float32 [4608], P('mp')
- down_grad: float32 [4608, 1152], P('mp')
- down_bias_grad: float32 [1152], replicated
Inputs may be any that keep to these rules, and one draw needn't show every extreme that they name: counts[g] is how many of the 16 sample slots of index g of dp hold a live sample (the first ones); at least one index holds 16. offset_index[i, j] depends only on the displacement between patches i and j on the 16 x 16 grid (patch p at row p // 16, column p mod 16); distinct displacements have distinct entries.
All inputs are finite; a program needn't handle non-finite values.
Results may differ from a plain program's by a relative error of at most 0.02.
The roundings to bfloat16 on the way count: a program that leaves them out, or rounds other values in their place, can miss the bound.
Values may be sent and summed in bfloat16 or wider, within the bound.
No kernel may reach another device: no remote copies, remote signals or barrier semaphores. Data moves between devices by JAX's collectives and lax.ppermute only.
A program may use at most 256 MiB of HBM per device.

v0:
```python
from functools import partial

import jax
import jax.numpy as jnp
from jax import lax
from jax.sharding import PartitionSpec as P

HS = 72


EPSILON = 1e-06
HIGHEST = lax.Precision.HIGHEST


def normalize(values):
    centred = values - jnp.mean(values, axis=-1, keepdims=True)
    inverse = lax.rsqrt(jnp.mean(centred * centred, axis=-1, keepdims=True) + EPSILON)
    return (centred * inverse, inverse)


def norm_back(grad_normed, normed, inverse):
    first_mean = jnp.mean(grad_normed, axis=-1, keepdims=True)
    second_mean = jnp.mean(grad_normed * normed, axis=-1, keepdims=True)
    return (grad_normed - first_mean - normed * second_mean) * inverse


def column_sums(left, right):
    return lax.dot_general(
        left, right, (((0,), (0,)), ((), ())), preferred_element_type=jnp.float32
    )


def times_transposed(left, right):
    return lax.dot_general(
        left, right, (((1,), (1,)), ((), ())), preferred_element_type=jnp.float32
    )


def index_blocks(offset_index):
    patches = offset_index.shape[0]
    query_rows = min(patches, max(1, 4096 // patches))
    block_count = patches // query_rows
    return offset_index.reshape(block_count, query_rows * patches)


def bias_lookup(bias_table, offset_index):
    patches = offset_index.shape[0]
    head_count = bias_table.shape[1]
    entries = jnp.arange(bias_table.shape[0], dtype=jnp.int32)

    def lookup_block(flat_index):
        selection = (flat_index[:, None] == entries[None, :]).astype(jnp.bfloat16)
        return jnp.dot(selection, bias_table, preferred_element_type=jnp.float32)

    looked = lax.map(lookup_block, index_blocks(offset_index))
    return jnp.transpose(looked.reshape(patches, patches, head_count), (2, 0, 1))


def table_accumulate(table_terms, offset_index, table_rows):
    blocks = index_blocks(offset_index)
    head_count = table_terms.shape[-1]
    term_blocks = table_terms.reshape(blocks.shape[0], blocks.shape[1], head_count)
    entries = jnp.arange(table_rows, dtype=jnp.int32)

    def add_block(total, inputs):
        flat_index, terms = inputs
        selection = (flat_index[:, None] == entries[None, :]).astype(jnp.float32)
        return (
            total + lax.dot_general(selection, terms, (((0,), (0,)), ((), ())), precision=HIGHEST),
            None,
        )

    total, _ = lax.scan(
        add_block, jnp.zeros((table_rows, head_count), jnp.float32), (blocks, term_blocks)
    )
    return total


def attention_core(rows_in, flat_weight, bias_vector, bias_table, offset_index, head_count):
    patches = offset_index.shape[0]
    sample_count = rows_in.shape[0] // patches
    head_width = head_count * HS
    projected = (
        jnp.dot(rows_in, flat_weight, preferred_element_type=jnp.float32) + bias_vector
    ).astype(jnp.bfloat16)
    projected = projected.reshape(sample_count, patches, 3, head_count, HS)
    query_block = projected[:, :, 0]
    key_block = projected[:, :, 1]
    value_block = projected[:, :, 2]
    position_bias = bias_lookup(bias_table, offset_index)
    raw_scores = jnp.einsum(
        "sqhe,skhe->shqk", query_block, key_block, preferred_element_type=jnp.float32
    )
    scores = raw_scores * HS ** (-0.5) + position_bias[None]
    log_total = jax.nn.logsumexp(scores, axis=-1, keepdims=True)
    soft_weights = jnp.exp(scores - log_total).astype(jnp.bfloat16)
    attended = jnp.einsum(
        "shqk,skhe->sqhe", soft_weights, value_block, preferred_element_type=jnp.float32
    )
    attended = attended.astype(jnp.bfloat16).reshape(sample_count * patches, head_width)
    return ((query_block, key_block, value_block, position_bias, log_total), attended)


def attention_back(saved, grad_attended, offset_index, table_rows):
    query_block, key_block, value_block, position_bias, log_total = saved
    sample_count, patches, head_count, _ = query_block.shape
    scale_factor = HS ** (-0.5)
    grad_attended = grad_attended.reshape(sample_count, patches, head_count, HS)
    raw_scores = jnp.einsum(
        "sqhe,skhe->shqk", query_block, key_block, preferred_element_type=jnp.float32
    )
    probs_float = jnp.exp(raw_scores * scale_factor + position_bias[None] - log_total)
    grad_soft = jnp.einsum(
        "sqhe,skhe->shqk", grad_attended, value_block, preferred_element_type=jnp.float32
    )
    grad_scores = probs_float * (
        grad_soft - jnp.sum(probs_float * grad_soft, axis=-1, keepdims=True)
    )
    grad_scores = grad_scores.astype(jnp.bfloat16)
    value_grad = jnp.einsum(
        "shqk,sqhe->skhe",
        probs_float.astype(jnp.bfloat16),
        grad_attended,
        preferred_element_type=jnp.float32,
    )
    query_grad = (
        jnp.einsum("shqk,skhe->sqhe", grad_scores, key_block, preferred_element_type=jnp.float32)
        * scale_factor
    )
    key_grad = (
        jnp.einsum("shqk,sqhe->skhe", grad_scores, query_block, preferred_element_type=jnp.float32)
        * scale_factor
    )
    grad_projected = jnp.stack([query_grad, key_grad, value_grad], axis=2).astype(jnp.bfloat16)
    grad_projected = grad_projected.reshape(sample_count * patches, 3 * head_count * HS)
    table_terms = jnp.transpose(jnp.sum(grad_scores.astype(jnp.float32), axis=0), (1, 2, 0))
    table_grad = table_accumulate(
        table_terms.reshape(patches * patches, head_count), offset_index, table_rows
    )
    return (grad_projected, table_grad)


def bias_sums(grad_projected, head_width):
    grad_blocks = grad_projected.astype(jnp.float32).reshape(grad_projected.shape[0], 3, head_width)
    return jnp.stack([jnp.sum(grad_blocks[:, 0], axis=0), jnp.sum(grad_blocks[:, 2], axis=0)])


def joined_bias(qv_values, head_width):
    qv_float = qv_values.astype(jnp.float32)
    return jnp.concatenate([qv_float[0], jnp.zeros((head_width,), jnp.float32), qv_float[1]])


def local(
    tokens,
    conditioning,
    counts,
    offset_index,
    modulator,
    modulator_bias,
    qkv_weight,
    qv_bias,
    offset_table,
    out_weight,
    out_bias,
    up_weight,
    up_bias,
    down_weight,
    down_bias,
    out_grad,
):
    model_width = tokens.shape[1]
    local_rows = tokens.shape[0]
    samples = conditioning.shape[0]
    patches = offset_index.shape[0]
    local_width = qkv_weight.shape[2]
    local_heads = local_width // HS
    table_rows = offset_table.shape[0]
    row_number = lax.axis_index("mp") * local_rows + jnp.arange(local_rows, dtype=jnp.int32)
    row_sample = row_number // patches
    selector = (row_sample[:, None] == jnp.arange(samples, dtype=jnp.int32)[None, :]).astype(
        jnp.float32
    )
    live_rows = (row_sample < counts[0]).astype(jnp.float32)[:, None]
    cond_float = conditioning.astype(jnp.float32)
    activated = jax.nn.silu(cond_float).astype(jnp.bfloat16)
    mod_part = jnp.dot(
        activated, modulator, preferred_element_type=jnp.float32
    ) + modulator_bias.astype(jnp.float32)
    modulation = lax.all_gather(mod_part, "mp", axis=1, tiled=True)
    mod_rows = jnp.dot(selector, modulation, precision=HIGHEST)
    shift_one, scale_one, gate_one, shift_two, scale_two, gate_two = [
        mod_rows[:, number * model_width : (number + 1) * model_width] for number in range(6)
    ]
    tokens_float = tokens.astype(jnp.float32)
    normed_one, inverse_one = normalize(tokens_float)
    input_one = (normed_one * (1.0 + scale_one) + shift_one).astype(jnp.bfloat16)
    gathered_one = lax.all_gather(input_one, "mp", axis=0, tiled=True)
    flat_qkv = qkv_weight.reshape(model_width, 3 * local_width)
    saved, attended = attention_core(
        gathered_one,
        flat_qkv,
        joined_bias(qv_bias, local_width),
        offset_table,
        offset_index,
        local_heads,
    )
    attn_branch = lax.psum_scatter(
        jnp.dot(attended, out_weight, preferred_element_type=jnp.float32),
        "mp",
        scatter_dimension=0,
        tiled=True,
    ) + out_bias.astype(jnp.float32)
    mid_tokens = tokens_float + gate_one * attn_branch
    normed_two, inverse_two = normalize(mid_tokens)
    input_two = (normed_two * (1.0 + scale_two) + shift_two).astype(jnp.bfloat16)
    gathered_two = lax.all_gather(input_two, "mp", axis=0, tiled=True)
    pre_act = jnp.dot(gathered_two, up_weight, preferred_element_type=jnp.float32) + up_bias.astype(
        jnp.float32
    )
    hidden = jax.nn.gelu(pre_act, approximate=True).astype(jnp.bfloat16)
    mlp_branch = lax.psum_scatter(
        jnp.dot(hidden, down_weight, preferred_element_type=jnp.float32).astype(jnp.bfloat16),
        "mp",
        scatter_dimension=0,
        tiled=True,
    ).astype(jnp.float32) + down_bias.astype(jnp.float32)
    final_rows = mid_tokens + gate_two * mlp_branch
    block_out = (final_rows * live_rows).astype(jnp.bfloat16)
    grad_final = out_grad.astype(jnp.float32) * live_rows
    mlp_grad = (gate_two * grad_final).astype(jnp.bfloat16)
    _, gelu_back = jax.vjp(partial(jax.nn.gelu, approximate=True), pre_act)
    grad_rows_two = lax.all_gather(mlp_grad, "mp", axis=0, tiled=True)
    down_grad = column_sums(hidden, grad_rows_two)
    grad_hidden = times_transposed(grad_rows_two, down_weight)
    grad_pre = gelu_back(grad_hidden)[0].astype(jnp.bfloat16)
    up_grad = column_sums(gathered_two, grad_pre)
    up_bias_grad = jnp.sum(grad_pre.astype(jnp.float32), axis=0)
    grad_input_two = lax.psum_scatter(
        times_transposed(grad_pre, up_weight).astype(jnp.bfloat16),
        "mp",
        scatter_dimension=0,
        tiled=True,
    ).astype(jnp.float32)
    grad_mid = grad_final + norm_back(grad_input_two * (1.0 + scale_two), normed_two, inverse_two)
    attn_grad = (gate_one * grad_mid).astype(jnp.bfloat16)
    grad_rows_one = lax.all_gather(attn_grad, "mp", axis=0, tiled=True)
    out_weight_grad = column_sums(attended, grad_rows_one)
    grad_attended = times_transposed(grad_rows_one, out_weight).astype(jnp.bfloat16)
    grad_projected, offset_table_grad = attention_back(
        saved, grad_attended, offset_index, table_rows
    )
    qkv_grad = column_sums(gathered_one, grad_projected).reshape(model_width, 3, local_width)
    qv_bias_grad = bias_sums(grad_projected, local_width)
    grad_input_one = lax.psum_scatter(
        times_transposed(grad_projected, flat_qkv).astype(jnp.bfloat16),
        "mp",
        scatter_dimension=0,
        tiled=True,
    ).astype(jnp.float32)
    tokens_grad = grad_mid + norm_back(grad_input_one * (1.0 + scale_one), normed_one, inverse_one)
    mod_grad_rows = jnp.concatenate(
        [
            grad_input_one,
            grad_input_one * normed_one,
            grad_mid * attn_branch,
            grad_input_two,
            grad_input_two * normed_two,
            grad_final * mlp_branch,
        ],
        axis=1,
    )
    mod_grad_local = lax.dot_general(
        selector, mod_grad_rows, (((0,), (0,)), ((), ())), precision=HIGHEST
    )
    mod_grad = lax.psum_scatter(
        mod_grad_local.astype(jnp.bfloat16), "mp", scatter_dimension=1, tiled=True
    )
    modulator_grad = column_sums(activated, mod_grad)
    modulator_bias_grad = jnp.sum(mod_grad.astype(jnp.float32), axis=0)
    act_grad_part = times_transposed(mod_grad, modulator)
    act_grad, out_bias_grad, down_bias_grad = (
        lax.psum(act_grad_part.astype(jnp.bfloat16), "mp").astype(jnp.float32),
        lax.psum(jnp.sum(attn_grad.astype(jnp.float32), axis=0).astype(jnp.bfloat16), "mp").astype(
            jnp.float32
        ),
        lax.psum(jnp.sum(mlp_grad.astype(jnp.float32), axis=0).astype(jnp.bfloat16), "mp").astype(
            jnp.float32
        ),
    )
    _, silu_back = jax.vjp(jax.nn.silu, cond_float)
    cond_grad = silu_back(act_grad)[0]
    totals = (
        lax.psum(modulator_grad.astype(jnp.bfloat16), "dp").astype(jnp.float32),
        lax.psum(modulator_bias_grad.astype(jnp.bfloat16), "dp").astype(jnp.float32),
        lax.psum(qkv_grad.astype(jnp.bfloat16), "dp").astype(jnp.float32),
        lax.psum(qv_bias_grad.astype(jnp.bfloat16), "dp").astype(jnp.float32),
        lax.psum(offset_table_grad.astype(jnp.bfloat16), "dp").astype(jnp.float32),
        lax.psum(out_weight_grad.astype(jnp.bfloat16), "dp").astype(jnp.float32),
        lax.psum(out_bias_grad.astype(jnp.bfloat16), "dp").astype(jnp.float32),
        lax.psum(up_grad.astype(jnp.bfloat16), "dp").astype(jnp.float32),
        lax.psum(up_bias_grad.astype(jnp.bfloat16), "dp").astype(jnp.float32),
        lax.psum(down_grad.astype(jnp.bfloat16), "dp").astype(jnp.float32),
        lax.psum(down_bias_grad.astype(jnp.bfloat16), "dp").astype(jnp.float32),
    )
    return (
        block_out,
        tokens_grad,
        cond_grad,
        totals[0],
        totals[1],
        totals[2],
        totals[3],
        totals[4],
        totals[5],
        totals[6],
        totals[7],
        totals[8],
        totals[9],
        totals[10],
    )


def solution(mesh):
    in_specs = (
        P(("dp", "mp"), None),
        P("dp", None),
        P("dp"),
        P(),
        P(None, "mp"),
        P("mp"),
        P(None, None, "mp"),
        P(None, "mp"),
        P(None, "mp"),
        P("mp", None),
        P(),
        P(None, "mp"),
        P("mp"),
        P("mp", None),
        P(),
        P(("dp", "mp"), None),
    )
    out_specs = (
        P(("dp", "mp"), None),
        P(("dp", "mp"), None),
        P("dp", None),
        P(None, "mp"),
        P("mp"),
        P(None, None, "mp"),
        P(None, "mp"),
        P(None, "mp"),
        P("mp", None),
        P(),
        P(None, "mp"),
        P("mp"),
        P("mp", None),
        P(),
    )
    return jax.shard_map(local, mesh=mesh, in_specs=in_specs, out_specs=out_specs, check_vma=False)
```

profile of v0, /device:TPU:0, one launch (start us, length us, event | category | flops | bytes accessed | tf_op | source)
XLA Modules:
  0.0 1794.9 jit_solution(14552597629582173609)
XLA Ops:
  11.3 32.9 %all-gather = f32[8,864,16]{1,2,0:T(8,128)S(1)} all-gather(f32[1,864,16]{1,2,0:T(8,128)S(1)} %fusion.40), channel_id=1, replica_groups=mesh['dp'=4,'mp'=8] {'mp'}, dimensions={0}, use_global_device_ids=true | all-gather | bytes 497664 | tf_op jit(solution)/shard_map/all_gather | solution.py:189
  59.8 88.4 %while.22 = (s32[]{:T(128)}, f32[16,4096,2]{1,0,2:T(8,128)}, s32[16,4096]{1,0:T(8,128)S(1)}, bf16[961,2]{0,1:T(2,128)(2,1)S(1)}, s32[]{:T(128)}, /*index=5*/s32[]{:T(128)}) while((s32[]{:T(128)}, f32[16,4096,2]{1,0,2:T(8,128)}, s32[16,4096]{1,0:T(8,128)S(1)}, bf16[961,2]{0,1:T(2,128)(2,1)S(1)}, s32[]{:T(128)}, ...), condition=%wide.region_3.4_spmd.clone, body=%wide.region_2.3_spmd.clone.sunk | while | flops 19681280 | bytes 216921 | solution.py:55
  152.4 45.8 %all-gather.6.cloned.1.call-done = bf16[4096,1152]{1,0:T(8,128)(2,1)} async-done(((bf16[512,1152]{1,0:T(8,128)(2,1)}), bf16[4096,1152]{1,0:T(8,128)(2,1)}) %all-gather.6.cloned.1.call-update) | async-done | bytes 9437200 | tf_op jit(solution)/shard_map/all_gather | solution.py:197
  198.1 8.6 add_convert_fusion
  219.4 8.0 fusion.75
  228.1 311.2 %reduce-scatter.8.cloned.1.call-done = f32[512,1152]{1,0:T(8,128)} async-done(((f32[4096,1152]{1,0:T(8,128)}), f32[512,1152]{1,0:T(8,128)}) %reduce-scatter.8.cloned.1.call-update) | async-done | bytes 2359312 | tf_op jit(solution)/shard_map/reduce_scatter | solution.py:207
  552.2 132.8 %all-gather.8.cloned.1.call-done = bf16[4096,1152]{1,0:T(8,128)(2,1)} async-done(((bf16[512,1152]{1,0:T(8,128)(2,1)}), bf16[4096,1152]{1,0:T(8,128)(2,1)}) %all-gather.8.cloned.1.call-update) | async-done | bytes 9437200 | tf_op jit(solution)/shard_map/all_gather | solution.py:216
  685.0 9.4 fusion.76
  698.0 12.4 convolution_convert_fusion.2
  710.5 113.4 %all-gather.10.cloned.1.call-done = bf16[4096,1152]{1,0:T(8,128)(2,1)} async-done(((bf16[512,1152]{1,0:T(8,128)(2,1)}), bf16[4096,1152]{1,0:T(8,128)(2,1)}) %all-gather.10.cloned.1.call-update) | async-done | bytes 9437200 | tf_op jit(solution)/shard_map/all_gather | solution.py:232
  823.9 16.6 fusion.68
  842.7 10.6 convolution_convert_fusion.1
  854.0 135.0 %reduce-scatter.10.cloned.1.call-done = bf16[512,1152]{1,0:T(8,128)(2,1)} async-done(((bf16[4096,1152]{1,0:T(8,128)(2,1)}), bf16[512,1152]{1,0:T(8,128)(2,1)}) %reduce-scatter.10.cloned.1.call-update) | async-done | bytes 1179664 | tf_op jit(solution)/shard_map/reduce_scatter | solution.py:221
  989.0 166.1 %reduce-scatter.12.cloned.1.call-done = bf16[512,1152]{1,0:T(8,128)(2,1)} async-done(((bf16[4096,1152]{1,0:T(8,128)(2,1)}), bf16[512,1152]{1,0:T(8,128)(2,1)}) %reduce-scatter.12.cloned.1.call-update) | async-done | bytes 1179664 | tf_op jit(solution)/shard_map/reduce_scatter | solution.py:238
  1165.5 137.1 %all-gather.12.cloned.1.call-done = bf16[4096,1152]{1,0:T(8,128)(2,1)} async-done(((bf16[512,1152]{1,0:T(8,128)(2,1)}), bf16[4096,1152]{1,0:T(8,128)(2,1)}) %all-gather.12.cloned.1.call-update) | async-done | bytes 9437200 | tf_op jit(solution)/shard_map/all_gather | solution.py:246
  1336.4 8.3 convolution_convert_fusion
  1344.8 11.7 convolution_convert_fusion.6
  1356.5 14.9 convolution_convert_fusion.7
  1372.6 10.5 fusion.21
  1383.1 123.5 %reduce-scatter.14.cloned.1.call-done = bf16[512,1152]{1,0:T(8,128)(2,1)} async-done(((bf16[4096,1152]{1,0:T(8,128)(2,1)}), bf16[512,1152]{1,0:T(8,128)(2,1)}) %reduce-scatter.14.cloned.1.call-update) | async-done | bytes 1179664 | tf_op jit(solution)/shard_map/reduce_scatter | solution.py:254
  1531.8 59.3 %reduce-scatter.16.cloned.1.call-done = bf16[864,16]{1,0:T(8,128)(2,1)} async-done(((bf16[6912,16]{1,0:T(8,128)(2,1)}), bf16[864,16]{1,0:T(8,128)(2,1)}) %reduce-scatter.16.cloned.1.call-update) | async-done | bytes 27664
  1594.0 115.8 %while.23 = (s32[]{:T(128)}, f32[961,2]{0,1:T(2,128)S(1)}, s32[16,4096]{1,0:T(8,128)}, f32[16,4096,2]{1,0,2:T(8,128)}, s32[]{:T(128)}, /*index=5*/s32[]{:T(128)}) while((s32[]{:T(128)}, f32[961,2]{0,1:T(2,128)S(1)}, s32[16,4096]{1,0:T(8,128)}, f32[16,4096,2]{1,0,2:T(8,128)}, s32[]{:T(128)}, /*index=5*/s32[]{:T(128)}) %tuple.93), condition=%wide.region_28.29_spmd.clone, body=%wide.region_27.28_spmd.clone.sunk | while | flops 98410240 | bytes 162927 | solution.py:73
  1726.9 35.3 %all-reduce = (bf16[16,1152]{1,0:T(8,128)(2,1)S(1)}, bf16[1152]{0:T(1024)(128)(2,1)S(1)}, bf16[1152]{0:T(1024)(128)(2,1)S(1)}) all-reduce(bf16[16,1152]{1,0:T(8,128)(2,1)S(1)} %convolution_convert_fusion.9, bf16[1152]{0:T(1024)(128)(2,1)S(1)} %copy-done.48, bf16[1152]{0:T(1024)(128)(2,1)S(1)} %copy-done.47), channel_id=1, replica_groups=mesh['dp'=4,'mp'=8] {'mp'}, use_global_device_ids=true, to_apply=%region_18.19 | all-reduce | flops 20736 | bytes 82944 | tf_op jit(solution)/shard_map/psum | solution.py:282
  1762.3 10.2 all-reduce.1
  (354 shorter events, 364.9 us)
Async XLA Ops:
  7.2 190.9 %all-gather.6.cloned.1.call-start = ((), (), s32[]{:S(2)}) async-start(), calls=%async_computation.5 | async-start | bytes 10616832 | tf_op jit(solution)/shard_map/all_gather | solution.py:197
  7.3 38.0 %copy-start.39 = (s32[512]{0:T(512)}, s32[512]{0:T(512)S(1)}, u32[]{:S(2)}) copy-start(s32[512]{0:T(512)S(1)} %add_select_fusion) | copy-start | bytes 6148
  8.9 43.2 %copy-start.43 = (f32[512]{0:T(512)}, f32[512]{0:T(512)S(1)}, u32[]{:S(2)}) copy-start(f32[512]{0:T(512)S(1)} %broadcast_multiply_fusion.5) | copy-start | bytes 6148
  10.7 41.5 %copy-start.45 = (f32[512]{0:T(512)}, f32[512]{0:T(512)S(1)}, u32[]{:S(2)}) copy-start(f32[512]{0:T(512)S(1)} %add_rsqrt_fusion.1) | copy-start | bytes 6148
  58.7 480.6 %reduce-scatter.8.cloned.1.call-start = ((), (), s32[]{:S(2)}) async-start(), calls=%async_computation.6 | async-start | bytes 21233664 | tf_op jit(solution)/shard_map/reduce_scatter | solution.py:207
  59.8 92.4 %copy-start.52 = (bf16[2,144]{1,0:T(2,128)(2,1)S(1)}, bf16[2,144]{1,0:T(2,128)(2,1)}, u32[]{:S(2)}) copy-start(bf16[2,144]{1,0:T(2,128)(2,1)} %param.27) | copy-start | bytes 1732
  148.2 58.6 %copy-start.35 = (s32[16,4096]{1,0:T(8,128)}, s32[16,4096]{1,0:T(8,128)S(1)}, u32[]{:S(2)}) copy-start(s32[16,4096]{1,0:T(8,128)S(1)} %get-tuple-element.311) | copy-start | bytes 786436
  227.5 457.6 %all-gather.8.cloned.1.call-start = ((), (), s32[]{:S(2)}) async-start(), calls=%async_computation.7 | async-start | bytes 10616832 | tf_op jit(solution)/shard_map/all_gather | solution.py:216
  228.1 314.1 %copy-start.41 = (f32[1152]{0:T(1024)}, f32[1152]{0:T(1024)S(1)}, u32[]{:S(2)}) copy-start(f32[1152]{0:T(1024)S(1)} %convert_element_type.200) | copy-start | bytes 13828
  547.7 276.2 %all-gather.10.cloned.1.call-start = ((), (), s32[]{:S(2)}) async-start(), calls=%async_computation.9 | async-start | bytes 10616832 | tf_op jit(solution)/shard_map/all_gather | solution.py:232
  552.2 436.9 %reduce-scatter.10.cloned.1.call-start = ((), (), s32[]{:S(2)}) async-start(), calls=%async_computation.8 | async-start | bytes 10616832 | tf_op jit(solution)/shard_map/reduce_scatter | solution.py:221
  552.2 271.7 %copy-start.50 = (f32[576]{0:T(1024)}, f32[576]{0:T(1024)S(1)}, u32[]{:S(2)}) copy-start(f32[576]{0:T(1024)S(1)} %convert_element_type.202) | copy-start | bytes 6916
  710.4 444.6 %reduce-scatter.12.cloned.1.call-start = ((), (), s32[]{:S(2)}) async-start(), calls=%async_computation.10 | async-start | bytes 10616832 | tf_op jit(solution)/shard_map/reduce_scatter | solution.py:238
  823.9 18.7 %copy-start.57 = (bf16[1152,576]{0,1:T(8,128)(2,1)S(1)}, bf16[1152,576]{0,1:T(8,128)(2,1)}, u32[]{:S(2)}) copy-start(bf16[1152,576]{0,1:T(8,128)(2,1)} %param.31) | copy-start | bytes 3981316
  853.3 449.3 %all-gather.12.cloned.1.call-start = ((), (), s32[]{:S(2)}) async-start(), calls=%async_computation.11 | async-start | bytes 10616832 | tf_op jit(solution)/shard_map/all_gather | solution.py:246
  1165.3 341.3 %reduce-scatter.14.cloned.1.call-start = ((), (), s32[]{:S(2)}) async-start(), calls=%async_computation.12 | async-start | bytes 10616832 | tf_op jit(solution)/shard_map/reduce_scatter | solution.py:254
  1344.8 246.3 %reduce-scatter.16.cloned.1.call-start = ((), (), s32[]{:S(2)}) async-start(), calls=%async_computation.13 | async-start | bytes 1990656
  1383.1 125.0 %copy-start.7 = (bf16[512,1152]{1,0:T(8,128)(2,1)S(1)}, bf16[512,1152]{1,0:T(8,128)(2,1)}, u32[]{:S(2)}) copy-start(bf16[512,1152]{1,0:T(8,128)(2,1)} %param.20) | copy-start | bytes 3538948
  1383.1 125.0 %copy-start.44 = (f32[512]{0:T(512)S(1)}, f32[512]{0:T(512)}, u32[]{:S(2)}) copy-start(f32[512]{0:T(512)} %copy-done.43) | copy-start | bytes 6148
  1383.1 125.0 %copy-start.46 = (f32[512]{0:T(512)S(1)}, f32[512]{0:T(512)}, u32[]{:S(2)}) copy-start(f32[512]{0:T(512)} %copy-done.45) | copy-start | bytes 6148
  1525.6 65.5 %copy-start.37 = (bf16[16,1152]{1,0:T(8,128)(2,1)S(1)}, bf16[16,1152]{1,0:T(8,128)(2,1)}, u32[]{:S(2)}) copy-start(bf16[16,1152]{1,0:T(8,128)(2,1)} %param.21) | copy-start | bytes 110596
  1525.6 251.3 %all-reduce.5.cloned.1.call-start = ((), (), s32[]{:S(2)}) async-start(), calls=%async_computation.14 | async-start | bytes 11943936 | tf_op jit(solution)/shard_map/psum | solution.py:293
  1594.0 115.8 %copy-start.23 = (bf16[16,2,72,256]{3,2,1,0:T(8,128)(2,1)S(1)}, bf16[16,2,72,256]{3,2,1,0:T(8,128)(2,1)}, u32[]{:S(2)}) copy-start(bf16[16,2,72,256]{3,2,1,0:T(8,128)(2,1)} %copy-done.22) | copy-start | bytes 3538948
  1724.7 37.6 %copy-start.55 = (bf16[576]{0:T(1024)(128)(2,1)S(1)}, bf16[576]{0:T(1024)(128)(2,1)}, u32[]{:S(2)}) copy-start(bf16[576]{0:T(1024)(128)(2,1)} %get-tuple-element.141) | copy-start | bytes 3460
  (50 other events, 195.9 us)
Sparse Core Ops, SparseCore 0:
  58.9 139.2 all-gather.5
  227.6 311.6 reduce-scatter.7
  547.8 137.1 all-gather.7
  687.6 136.2 all-gather.9
  827.4 161.6 reduce-scatter.9
  992.5 162.5 reduce-scatter.11
  1165.4 137.1 all-gather.11
  1344.9 161.6 reduce-scatter.13
  1525.7 65.3 reduce-scatter.15
  1595.0 114.3 all-reduce.4
where the time goes:
time: 1800 us; the launch traced here: 1790 us
  waiting for transfers between devices  1220 us (68%)
  matrix products  305 us (17%)
  local copies, waits for them, and re-layouts  112 us (6%)
  blocking collectives  78.4 us (4%)
  other arithmetic  59 us (3%)
    reduce_scatter x1, waiting for transfers between devices, local(): lax.psum_scatter(jnp.dot(attended, out_weight, preferred_element_type=jnp...  311 us
    reduce_scatter x1, waiting for transfers between devices, local(): lax.psum_scatter(times_transposed(grad_pre, up_weight).astype(jnp.bfloat1...  166 us
    all_gather x1, waiting for transfers between devices, local(): grad_rows_one = lax.all_gather(attn_grad, 'mp', axis=0, tiled=True)  137 us
    reduce_scatter x1, waiting for transfers between devices, local(): lax.psum_scatter(jnp.dot(hidden, down_weight, preferred_element_type=jnp....  135 us
    all_gather x1, waiting for transfers between devices, local(): gathered_two = lax.all_gather(input_two, 'mp', axis=0, tiled=True)  133 us
    reduce_scatter x1, waiting for transfers between devices, local(): lax.psum_scatter(times_transposed(grad_projected, flat_qkv).astype(jnp.bf...  123 us
    all_gather x1, waiting for transfers between devices, local(): grad_rows_two = lax.all_gather(mlp_grad, 'mp', axis=0, tiled=True)  113 us
    dot_general x16, matrix products, add_block(): lax.dot_general(selection, terms, (((0,), (0,)), ((), ())), precision=HIG...  84.7 us
  transfers between devices with their start and end apart: 10, of which 9 were waited for; matrix products, arithmetic and copies ran while one was open for 18% of the time, Pallas kernels for 0%

commit v1 on v0

v1 whole, which is shorter than its diff:
```python
from functools import partial

import jax
import jax.numpy as jnp
from jax import lax
from jax.experimental import pallas as pl
from jax.experimental.pallas import tpu as pltpu
from jax.sharding import PartitionSpec as P

HS = 72
EPSILON = 1e-06
HIGHEST = lax.Precision.HIGHEST
BOTH = ("dp", "mp")
VMEM_BYTES = 44 * 2**20
BF16 = jnp.bfloat16
F32 = jnp.float32


def low(value):
    return value.astype(BF16)


def low_sum(*values):
    total = values[0].astype(F32)
    for value in values[1:]:
        total = total + value.astype(F32)
    return low(total)


class PairPlan:
    def __init__(self, mesh):
        self.zs = mesh.shape["mp"] // 2
        zs = self.zs
        self.core = self.moves(lambda y, c, z, x: (y, 1 - c, z, x))
        self.across_x = self.moves(lambda y, c, z, x: (y, c, z, 1 - x))
        self.across_y = self.moves(lambda y, c, z, x: (1 - y, c, z, x))
        self.up = self.moves(lambda y, c, z, x: (y, c, (z + 1) % zs, x))
        self.down = self.moves(lambda y, c, z, x: (y, c, (z - 1) % zs, x))

    def moves(self, target):
        def number(y, c, z, x):
            return ((y * 2 + c) * self.zs + z) * 2 + x

        places = [(y, c, z, x) for y in (0, 1) for c in (0, 1) for z in range(self.zs) for x in (0, 1)]
        return [(number(*place), number(*target(*place))) for place in places]

    def here(self):
        dp, mp = lax.axis_index("dp"), lax.axis_index("mp")
        return dp // 2, dp % 2, mp // 2, mp % 2

    def first_half(self):
        return self.here()[0]

    def move(self, value, way):
        return lax.ppermute(value, BOTH, way)

    def turned(self, values, halves):
        y, c, z, x = self.here()
        places = jnp.arange(self.zs)
        pick = (places[:, None] + places[None, :]) % self.zs == z
        pick = pick.reshape(pick.shape + (1,) * (values.ndim - 1))
        values = jnp.sum(jnp.where(pick, values[None], jnp.zeros_like(values[None])), axis=1)
        values = jnp.where(x == 0, values, values[:, ::-1])
        values = jnp.where(c == 0, values, values[:, :, ::-1])
        if halves:
            values = jnp.where(y == 0, values, values[:, :, :, ::-1])
        return values

    def to_own(self, values, halves):
        rest = values.shape[1:]
        lead = (self.zs, 2, 2, 2) if halves else (self.zs, 2, 2)
        split = values.reshape(lead + (-1,) + rest)
        split = self.turned(split, halves)
        split = split.transpose((2, 1, 0) + tuple(range(3, split.ndim)))
        return split.reshape((2, values.shape[0] // 2) + rest)

    def to_whole(self, values, halves):
        rest = values.shape[2:]
        lead = (2, 2, self.zs, 2) if halves else (2, 2, self.zs)
        split = values.reshape(lead + (-1,) + rest)
        split = split.transpose((2, 1, 0) + tuple(range(3, split.ndim)))
        return self.turned(split, halves).reshape((-1,) + rest)

    def gather(self, shard, light):
        y, c, _, _ = self.here()
        rows, width = shard.shape
        shard = shard.reshape(2, 2, rows // 4, width)
        mine = lax.dynamic_index_in_dim(shard, c, 0, keepdims=False)
        m0 = lax.dynamic_index_in_dim(mine, y, 0, keepdims=False)
        n0 = lax.dynamic_index_in_dim(mine, 1 - y, 0, keepdims=False)
        m1 = self.move(m0, self.up)
        m3 = self.move(m0, self.down)
        m2 = self.move(m1, self.up)
        first = [m0, m1, m2, m3]
        if light:
            second = [n0] + [self.move(piece, self.across_y) for piece in first[1:]]
        else:
            n1 = self.move(n0, self.up)
            n3 = self.move(n0, self.down)
            n2 = self.move(n3, self.down)
            second = [n0, n1, n2, n3]
        first += [self.move(piece, self.across_x) for piece in first]
        second += [self.move(piece, self.across_y) for piece in first[self.zs :]]
        pieces = [piece for pair in zip(first, second) for piece in pair]
        own = jnp.concatenate(pieces, axis=0)
        return own, self.move(own, self.core)

    def scatter(self, other, own_sum, light):
        y, c, _, _ = self.here()
        total = own_sum(self.move(other, self.core))
        rows, width = total.shape
        total = total.reshape(2, self.zs, 2, rows // (4 * self.zs), width)
        near, far = total[0], total[1]
        far_sum = low_sum(far[:, 0], self.move(far[:, 1], self.across_y))
        m = low_sum(near[:, 0], self.move(far_sum, self.across_x))
        n = near[:, 1]
        if light:
            back = self.move(n[1:], self.across_y)
            m = jnp.concatenate([m[:1], low_sum(m[1:], back)])
            n_done = n[0]
        else:
            n3 = low_sum(n[3], self.move(n[2], self.up))
            n_done = low_sum(n[0], self.move(n[1], self.down), self.move(n3, self.up))
        m1 = low_sum(m[1], self.move(m[2], self.down))
        m_done = low_sum(m[0], self.move(m[3], self.up), self.move(m1, self.down))
        crossed = self.move(jnp.stack([n_done, m_done]), self.across_y)
        done = low_sum(jnp.stack([m_done, n_done]), crossed)
        done = jnp.where(y == 0, done, done[::-1])
        done = jnp.stack([done, self.move(done, self.core)])
        done = jnp.where(c == 0, done, done[::-1]).astype(F32)
        return done.reshape(rows // (2 * self.zs) * 2, width)


class PlainPlan:
    def first_half(self):
        return jnp.int32(0)

    def to_own(self, values, halves):
        return values.reshape((2, -1) + values.shape[1:])

    def to_whole(self, values, halves):
        return values.reshape((-1,) + values.shape[2:])

    def gather(self, shard, light):
        full = lax.all_gather(shard, "mp", axis=0, tiled=True)
        return jnp.split(full, 2, axis=0)

    def scatter(self, other, own_sum, light):
        full = jnp.concatenate([own_sum(jnp.zeros_like(other)), other], axis=0)
        part = lax.psum_scatter(full, "mp", scatter_dimension=0, tiled=True)
        return lax.psum(part, "dp").astype(F32)


def dot_nt(left, right):
    return lax.dot_general(left, right, (((1,), (1,)), ((), ())), preferred_element_type=F32)


def dot_tn(left, right):
    return lax.dot_general(left, right, (((0,), (0,)), ((), ())), preferred_element_type=F32)


def dot_nn(left, right):
    return lax.dot_general(left, right, (((1,), (0,)), ((), ())), preferred_element_type=F32)


def forward_kernel(half, x_ref, w_ref, b_ref, window_ref, qk_ref, va_ref, soft_ref, sum_ref):
    first = half[0]
    samples, patches = soft_ref.shape[1], soft_ref.shape[2]
    grid_side = window_ref.shape[1]
    x = x_ref[...]
    w_qk = w_ref[0, first]
    w_vo = w_ref[0, 1 - first]
    qk = low(dot_nt(x, w_qk) + b_ref[0, 0:1])
    vo = low(dot_nt(x, w_vo) + b_ref[0, 1:2])
    qk_ref[0] = qk
    queries, keys, values = qk[:, :HS], qk[:, HS:], vo[:, :HS]
    window = window_ref[0]
    width = window.shape[1]
    bias = jnp.concatenate(
        [
            pltpu.roll(window, (width - (grid_side - 1 - row) * grid_side) % width, 1)[:, :patches]
            for row in range(grid_side)
        ],
        axis=0,
    )
    joined = []
    for sample in range(samples):
        rows = slice(sample * patches, (sample + 1) * patches)
        scores = dot_nt(queries[rows], keys[rows]) * HS ** (-0.5) + bias
        powers = jnp.exp(scores - jnp.max(scores, axis=-1, keepdims=True))
        soft = low(powers * (1.0 / jnp.sum(powers, axis=-1, keepdims=True)))
        soft_ref[0, sample] = soft
        attended = low(dot_nn(soft, values[rows]))
        joined.append(jnp.concatenate([values[rows], attended], axis=1))
    joined = jnp.concatenate(joined, axis=0)
    va_ref[0] = joined
    lane = lax.broadcasted_iota(jnp.int32, joined.shape, 1)
    part = dot_nn(jnp.where(lane < HS, jnp.zeros_like(joined), joined), w_vo)

    @pl.when(pl.program_id(0) == 0)
    def _():
        sum_ref[...] = part

    @pl.when(pl.program_id(0) > 0)
    def _():
        sum_ref[...] += part


def backward_kernel(
    half, x_ref, g_ref, w_ref, qk_ref, va_ref, soft_ref, dw_ref, db_ref, dwindow_ref, sum_ref
):
    first = half[0]
    samples, patches = soft_ref.shape[1], soft_ref.shape[2]
    grid_side = dwindow_ref.shape[1]
    x = x_ref[...]
    grad = g_ref[...]
    w_qk = w_ref[0, first]
    w_vo = w_ref[0, 1 - first]
    grad_attended = low(dot_nt(grad, w_vo))[:, HS:]
    qk = qk_ref[0]
    va = va_ref[0]
    queries, keys, values = qk[:, :HS], qk[:, HS:], va[:, :HS]
    score_sum = None
    grads_qk, grads_v = [], []
    for sample in range(samples):
        rows = slice(sample * patches, (sample + 1) * patches)
        soft = soft_ref[0, sample]
        grad_here = grad_attended[rows]
        grad_soft = dot_nt(grad_here, values[rows])
        grads_v.append(dot_tn(soft, grad_here))
        weighted = soft.astype(F32) * grad_soft
        grad_scores = weighted - soft.astype(F32) * jnp.sum(weighted, axis=-1, keepdims=True)
        grad_scores = low(grad_scores)
        wide = grad_scores.astype(F32)
        score_sum = wide if score_sum is None else score_sum + wide
        grad_q = dot_nn(grad_scores, keys[rows]) * HS ** (-0.5)
        grad_k = dot_tn(grad_scores, queries[rows]) * HS ** (-0.5)
        grads_qk.append(jnp.concatenate([grad_q, grad_k], axis=1))
    grad_qk = low(jnp.concatenate(grads_qk, axis=0))
    grad_v = low(jnp.concatenate(grads_v, axis=0))
    grad_vo = jnp.concatenate([grad_v, jnp.zeros_like(grad_v)], axis=1)
    dw_qk = low(dot_tn(grad_qk, x))
    dw_vo = low(jnp.concatenate([dot_tn(grad_v, x), dot_tn(va[:, HS:], grad)], axis=0))
    dw_ref[0, 0] = lax.select(first == 0, dw_qk, dw_vo)
    dw_ref[0, 1] = lax.select(first == 0, dw_vo, dw_qk)
    db_ref[0, 0:1] = jnp.sum(grad_qk.astype(F32), axis=0, keepdims=True)
    db_ref[0, 1:2] = jnp.sum(grad_vo.astype(F32), axis=0, keepdims=True)
    width = dwindow_ref.shape[2]
    window = jnp.zeros((grid_side, width), F32)
    blank = jnp.zeros((grid_side, width - patches), F32)
    for row in range(grid_side):
        band = score_sum[row * grid_side : (row + 1) * grid_side]
        window = window + pltpu.roll(
            jnp.concatenate([band, blank], axis=1), (grid_side - 1 - row) * grid_side, 1
        )
    dwindow_ref[0] = window
    part = dot_nn(grad_qk, w_qk) + dot_nn(grad_vo, w_vo)

    @pl.when(pl.program_id(0) == 0)
    def _():
        sum_ref[...] = part

    @pl.when(pl.program_id(0) > 0)
    def _():
        sum_ref[...] += part


def same(shape):
    return pl.BlockSpec(shape, lambda head, half: (0,) * len(shape))


def per_head(shape):
    return pl.BlockSpec((1,) + shape, lambda head, half: (head,) + (0,) * len(shape))


def attention_forward(half, rows_in, weights, bias, windows, patches):
    heads = weights.shape[0]
    count, width = rows_in.shape
    samples = count // patches
    flops = heads * 2 * count * (width * 6 * HS + patches * 2 * HS)
    return pl.pallas_call(
        forward_kernel,
        grid_spec=pltpu.PrefetchScalarGridSpec(
            num_scalar_prefetch=1,
            grid=(heads,),
            in_specs=[
                same(rows_in.shape),
                per_head(weights.shape[1:]),
                per_head(bias.shape[1:]),
                per_head(windows.shape[1:]),
            ],
            out_specs=[
                per_head((count, 2 * HS)),
                per_head((count, 2 * HS)),
                per_head((samples, patches, patches)),
                same(rows_in.shape),
            ],
        ),
        out_shape=[
            jax.ShapeDtypeStruct((heads, count, 2 * HS), BF16),
            jax.ShapeDtypeStruct((heads, count, 2 * HS), BF16),
            jax.ShapeDtypeStruct((heads, samples, patches, patches), BF16),
            jax.ShapeDtypeStruct((count, width), F32),
        ],
        compiler_params=pltpu.CompilerParams(vmem_limit_bytes=VMEM_BYTES),
        cost_estimate=pl.CostEstimate(
            flops=2 * flops, bytes_accessed=20 * 2**20, transcendentals=heads * count * patches
        ),
    )(half, rows_in, weights, bias, windows)


def attention_backward(half, rows_in, grad, weights, saved, window_shape, patches):
    heads = weights.shape[0]
    count, width = rows_in.shape
    samples = count // patches
    qk, va, soft = saved
    flops = heads * 2 * count * (width * 14 * HS + patches * 5 * HS)
    return pl.pallas_call(
        backward_kernel,
        grid_spec=pltpu.PrefetchScalarGridSpec(
            num_scalar_prefetch=1,
            grid=(heads,),
            in_specs=[
                same(rows_in.shape),
                same(grad.shape),
                per_head(weights.shape[1:]),
                per_head((count, 2 * HS)),
                per_head((count, 2 * HS)),
                per_head((samples, patches, patches)),
            ],
            out_specs=[
                per_head(weights.shape[1:]),
                per_head((2, 2 * HS)),
                per_head(window_shape),
                same(rows_in.shape),
            ],
        ),
        out_shape=[
            jax.ShapeDtypeStruct(weights.shape, BF16),
            jax.ShapeDtypeStruct((heads, 2, 2 * HS), F32),
            jax.ShapeDtypeStruct((heads,) + window_shape, F32),
            jax.ShapeDtypeStruct((count, width), F32),
        ],
        compiler_params=pltpu.CompilerParams(vmem_limit_bytes=VMEM_BYTES),
        cost_estimate=pl.CostEstimate(
            flops=2 * flops, bytes_accessed=30 * 2**20, transcendentals=0
        ),
    )(half, rows_in, grad, weights, qk, va, soft)


def displacement_entries(offset_index):
    side = int(round(offset_index.shape[0] ** 0.5))
    by_place = offset_index.reshape(side, side, side, side)
    rows = jnp.concatenate(
        [by_place[0, :, :0:-1, :].transpose(1, 0, 2), by_place[:, :, 0, :]], axis=0
    )
    return jnp.concatenate([rows[:, 0, :0:-1], rows[:, :, 0]], axis=1)


def column_selector(side):
    places = jnp.arange(side)
    shift = places[:, None] - places[None, :] + side - 1
    return jnp.arange(2 * side - 1)[:, None] == shift.reshape(1, side * side)


def table_windows(table, entries):
    span = entries.shape[0]
    side = (span + 1) // 2
    heads = table.shape[1]
    pick = entries.reshape(-1, 1) == jnp.arange(table.shape[0])[None, :]
    ordered = jnp.dot(low(pick), table, preferred_element_type=F32)
    ordered = ordered.reshape(span, span, heads)[::-1].transpose(2, 0, 1)
    spread = jnp.dot(low(ordered).reshape(-1, span), low(column_selector(side)), preferred_element_type=F32)
    spread = spread.reshape(heads, span, side, side).transpose(0, 2, 1, 3)
    spread = spread.reshape(heads, side, span * side)
    return jnp.pad(spread, ((0, 0), (0, 0), (0, side)))


def table_from_windows(windows, entries, table_rows):
    span = entries.shape[0]
    heads, side, _ = windows.shape
    spread = windows[:, :, : span * side].reshape(heads, side, span, side).transpose(0, 2, 1, 3)
    spread = spread.reshape(heads * span, side * side)
    ordered = jnp.dot(spread, column_selector(side).astype(F32).T, precision=HIGHEST)
    ordered = ordered.reshape(heads, span, span)[:, ::-1].reshape(heads, span * span)
    pick = entries.reshape(-1, 1) == jnp.arange(table_rows)[None, :]
    return jnp.dot(ordered, pick.astype(F32), precision=HIGHEST)


def normalize(values):
    centred = values - jnp.mean(values, axis=-1, keepdims=True)
    inverse = lax.rsqrt(jnp.mean(centred * centred, axis=-1, keepdims=True) + EPSILON)
    return (centred * inverse, inverse)


def norm_back(grad_normed, normed, inverse):
    first_mean = jnp.mean(grad_normed, axis=-1, keepdims=True)
    second_mean = jnp.mean(grad_normed * normed, axis=-1, keepdims=True)
    return (grad_normed - first_mean - normed * second_mean) * inverse


def attention_rows(qkv_weight, out_weight):
    width, _, local_width = qkv_weight.shape
    heads = local_width // HS
    qkv = qkv_weight.reshape(width, 3, heads, HS).transpose(2, 1, 3, 0)
    out = out_weight.reshape(heads, 1, HS, width)
    return jnp.concatenate([qkv, out], axis=1).reshape(heads * 4 * HS, width)


def local(
    plan,
    tokens,
    conditioning,
    counts,
    offset_index,
    modulator,
    modulator_bias,
    qkv_weight,
    qv_bias,
    offset_table,
    out_weight,
    out_bias,
    up_weight,
    up_bias,
    down_weight,
    down_bias,
    out_grad,
):
    rows, width = tokens.shape
    patches = offset_index.shape[0]
    samples = rows // patches
    group_samples = conditioning.shape[0]
    shards = group_samples // samples
    columns = modulator.shape[1]
    local_width = qkv_weight.shape[2]
    local_heads = local_width // HS
    table_rows = offset_table.shape[0]
    local_units = up_weight.shape[1]
    heads = local_heads * shards

    half = plan.first_half().reshape(1)
    attn_w = plan.gather(attention_rows(qkv_weight, out_weight), True)
    up_w = plan.gather(up_weight.T, False)
    down_w = plan.gather(down_weight, False)

    small = jnp.concatenate([qv_bias.reshape(-1), offset_table.reshape(-1), up_bias])
    small = lax.all_gather(small, "mp", axis=0)
    cut_one, cut_two = 2 * local_width, 2 * local_width + table_rows * local_heads
    all_qv = small[:, :cut_one].reshape(shards, 2, local_heads, HS).transpose(0, 2, 1, 3)
    all_qv = all_qv.reshape(heads, 2, HS).astype(F32)
    all_qv = jnp.concatenate([all_qv, jnp.zeros_like(all_qv)], axis=2)
    head_bias = plan.to_own(all_qv, False)
    table = small[:, cut_one:cut_two].reshape(shards, table_rows, local_heads)
    table = table.transpose(1, 0, 2).reshape(table_rows, heads)
    entries = displacement_entries(offset_index)
    windows = plan.to_own(table_windows(table, entries), False)
    up_biases = plan.to_own(small[:, cut_two:].reshape(-1).astype(F32), True)

    cond_float = conditioning.astype(F32)
    activated = low(jax.nn.silu(cond_float))
    mod_part = jnp.dot(activated, modulator, preferred_element_type=F32) + modulator_bias.astype(F32)
    mod_own = lax.all_to_all(mod_part.reshape(shards, samples, columns), "mp", 0, 0)
    mod_own = mod_own.transpose(1, 0, 2).reshape(samples, 6, 1, width)
    shift_one, scale_one, gate_one, shift_two, scale_two, gate_two = [mod_own[:, n] for n in range(6)]
    all_activated = lax.all_gather(activated, "dp", axis=0, tiled=True)

    sample_number = lax.axis_index("mp") * samples + jnp.arange(samples, dtype=jnp.int32)
    live = (sample_number < counts[0]).astype(F32)[:, None, None]

    by_sample = (samples, patches, width)
    flat = (rows, width)
    tokens_float = tokens.reshape(by_sample).astype(F32)
    normed_one, inverse_one = normalize(tokens_float)
    input_one = low(normed_one * (1.0 + scale_one) + shift_one).reshape(flat)

    head_shape = (heads // 2, 2, 2 * HS, width)
    attn_w = [part.reshape(head_shape) for part in attn_w]
    saved = []
    attn_branch = out_bias.astype(F32)
    for part in range(2):
        *kept, branch = attention_forward(
            half, input_one, attn_w[part], head_bias[part], windows[part], patches
        )
        saved.append(kept)
        attn_branch = attn_branch + branch.reshape(by_sample)
    mid_tokens = tokens_float + gate_one * attn_branch
    normed_two, inverse_two = normalize(mid_tokens)
    input_two = low(normed_two * (1.0 + scale_two) + shift_two).reshape(flat)

    grad_final = out_grad.reshape(by_sample).astype(F32) * live
    mlp_grad = low(gate_two * grad_final).reshape(flat)

    pre_act = [dot_nt(input_two, up_w[part]) + up_biases[part] for part in range(2)]
    hidden = [low(jax.nn.gelu(value, approximate=True)) for value in pre_act]
    down_shard = plan.scatter(
        low(dot_tn(hidden[1], mlp_grad)),
        lambda came: low(dot_tn(hidden[0], mlp_grad) + came.astype(F32)),
        False,
    )
    mlp_branch = dot_nn(hidden[0], down_w[0]) + dot_nn(hidden[1], down_w[1])
    mlp_branch = (mlp_branch + down_bias.astype(F32)).reshape(by_sample)
    block_out = low((mid_tokens + gate_two * mlp_branch) * live).reshape(flat)

    grad_pre = []
    for part in range(2):
        _, gelu_back = jax.vjp(partial(jax.nn.gelu, approximate=True), pre_act[part])
        grad_pre.append(low(gelu_back(dot_nt(mlp_grad, down_w[part]))[0]))
    grad_input_two = dot_nn(grad_pre[0], up_w[0]) + dot_nn(grad_pre[1], up_w[1])
    grad_input_two = grad_input_two.reshape(by_sample)
    up_shard = plan.scatter(
        low(dot_tn(grad_pre[1], input_two)),
        lambda came: low(dot_tn(grad_pre[0], input_two) + came.astype(F32)),
        False,
    )
    grad_mid = grad_final + norm_back(grad_input_two * (1.0 + scale_two), normed_two, inverse_two)
    attn_grad = low(gate_one * grad_mid).reshape(flat)

    window_shape = windows.shape[2:]
    back = [None, None]
    for part in (1, 0):
        back[part] = attention_backward(
            half, input_one, attn_grad, attn_w[part], saved[part], window_shape, patches
        )
    attn_rows = (heads // 2 * 4 * HS, width)
    attn_shard = plan.scatter(
        back[1][0].reshape(attn_rows),
        lambda came: low_sum(back[0][0].reshape(attn_rows), came),
        True,
    )
    grad_input_one = (back[0][3] + back[1][3]).reshape(by_sample)
    tokens_grad = grad_mid + norm_back(grad_input_one * (1.0 + scale_one), normed_one, inverse_one)

    mod_grad = jnp.stack(
        [
            jnp.sum(value, axis=1)
            for value in (
                grad_input_one,
                grad_input_one * normed_one,
                grad_mid * attn_branch,
                grad_input_two,
                grad_input_two * normed_two,
                grad_final * mlp_branch,
            )
        ],
        axis=1,
    )
    mod_grad = low(mod_grad).reshape(samples, shards, columns).transpose(1, 0, 2)
    mod_grad = lax.all_to_all(mod_grad, "mp", 0, 0).reshape(group_samples, columns)
    act_grad = lax.psum(low(dot_nt(mod_grad, modulator)), "mp").astype(F32)
    _, silu_back = jax.vjp(jax.nn.silu, cond_float)
    cond_grad = silu_back(act_grad)[0]
    all_mod_grad = lax.all_gather(mod_grad, "dp", axis=0, tiled=True)
    modulator_grad = dot_tn(all_activated, all_mod_grad)
    modulator_bias_grad = jnp.sum(all_mod_grad.astype(F32), axis=0)

    head_grads = plan.to_whole(jnp.stack([back[0][1], back[1][1]]), False)[:, :, :HS]
    window_grads = plan.to_whole(jnp.stack([back[0][2], back[1][2]]), False)
    table_grads = table_from_windows(window_grads, entries, table_rows)
    up_bias_grads = jnp.stack([jnp.sum(part.astype(F32), axis=0) for part in grad_pre])
    up_bias_grads = plan.to_whole(up_bias_grads, True)
    totals = lax.psum(
        jnp.concatenate(
            [
                head_grads.reshape(-1),
                table_grads.reshape(-1),
                up_bias_grads,
                jnp.sum(attn_grad.astype(F32), axis=0),
                jnp.sum(mlp_grad.astype(F32), axis=0),
            ]
        ),
        BOTH,
    )
    place = lax.axis_index("mp")

    def my_part(start, size):
        return lax.dynamic_slice_in_dim(totals, start + place * size, size)

    head_size = 2 * heads * HS
    table_size = heads * table_rows
    units = shards * local_units
    qv_bias_grad = my_part(0, head_size // shards).reshape(local_heads, 2, HS)
    qv_bias_grad = qv_bias_grad.transpose(1, 0, 2).reshape(2, local_width)
    offset_table_grad = my_part(head_size, table_size // shards).reshape(local_heads, table_rows).T
    up_bias_grad = my_part(head_size + table_size, local_units)
    tail = head_size + table_size + units
    out_bias_grad = totals[tail : tail + width]
    down_bias_grad = totals[tail + width :]

    attn_shard = attn_shard.reshape(local_heads, 4, HS, width)
    qkv_grad = attn_shard[:, :3].transpose(3, 1, 0, 2).reshape(width, 3, local_width)
    out_weight_grad = attn_shard[:, 3].reshape(local_width, width)
    return (
        block_out,
        tokens_grad.reshape(flat),
        cond_grad,
        modulator_grad,
        modulator_bias_grad,
        qkv_grad,
        qv_bias_grad,
        offset_table_grad,
        out_weight_grad,
        out_bias_grad,
        up_shard.T,
        up_bias_grad,
        down_shard,
        down_bias_grad,
    )


def solution(mesh):
    known = (mesh.shape["dp"], mesh.shape["mp"]) == (4, 8)
    plan = PairPlan(mesh) if known else PlainPlan()
    in_specs = (
        P(("dp", "mp"), None),
        P("dp", None),
        P("dp"),
        P(),
        P(None, "mp"),
        P("mp"),
        P(None, None, "mp"),
        P(None, "mp"),
        P(None, "mp"),
        P("mp", None),
        P(),
        P(None, "mp"),
        P("mp"),
        P("mp", None),
        P(),
        P(("dp", "mp"), None),
    )
    out_specs = (
        P(("dp", "mp"), None),
        P(("dp", "mp"), None),
        P("dp", None),
        P(None, "mp"),
        P("mp"),
        P(None, None, "mp"),
        P(None, "mp"),
        P(None, "mp"),
        P("mp", None),
        P(),
        P(None, "mp"),
        P("mp"),
        P("mp", None),
        P(),
    )
    return jax.shard_map(
        partial(local, plan), mesh=mesh, in_specs=in_specs, out_specs=out_specs, check_vma=False
    )
```

time: 1800 us -> 914 us (0.51)
  waiting for transfers between devices: 1220 us -> 334 us
  matrix products: 305 us -> 104 us
  Pallas kernels: 0 us -> 99.1 us
  starting transfers between devices: 0.59 us -> 93.9 us
    reduce_scatter x4 -> x0, waiting for transfers between devices: 736 us -> none  [the longest x1 311 us: local(): lax.psum_scatter(jnp.dot(attended, out_weight, preferred_element_type=jnp...]
    all_gather x4 -> x0, waiting for transfers between devices: 429 us -> none  [the longest x1 137 us: local(): grad_rows_one = lax.all_gather(attn_grad, 'mp', axis=0, tiled=True)]
    ppermute x0 -> x76, waiting for transfers between devices: none -> 271 us  [move(): return lax.ppermute(value, BOTH, way)]
    dot_general x55 -> x19, matrix products: 305 us -> 104 us  [the longest x5 32.7 us: dot_nt(): lax.dot_general(left, right, (((1,), (1,)), ((), ())), preferred_element_...]
    pallas_call x0 -> x4, Pallas kernels: none -> 99.1 us  [the longest x2 60.8 us: attention_backward(): pl.pallas_call(backward_kernel, grid_spec=pltpu.PrefetchScalarGridSpec(nu...]
    ppermute x0 -> x76, starting transfers between devices: none -> 83.9 us  [move(): return lax.ppermute(value, BOTH, way)]
    psum x1, waiting for transfers between devices: 0.01 us -> 63.1 us  [local(): lax.psum(jnp.concatenate([head_grads.reshape(-1), table_grads.reshape(-1)...]
    unnamed x11 -> x1, waiting for transfers between devices: 59.4 us -> 0.02 us
  transfers between devices with their start and end apart: 10 -> 79, of which waited for: 9 -> 38; matrix products, arithmetic and copies ran while one was open for 18% -> 20% of each run, Pallas kernels for 0% -> 4%
where the time goes in v1:
time: 914 us; the launch traced here: 906 us
  waiting for transfers between devices  334 us (37%)
  local copies, waits for them, and re-layouts  113 us (12%)
  matrix products  104 us (11%)
  Pallas kernels  99.1 us (11%)
  blocking collectives  94.6 us (10%)
  starting transfers between devices  93.9 us (10%)
  other arithmetic  50.8 us (6%)
  between operations  17.2 us (2%)
    ppermute x76, waiting for transfers between devices, move(): return lax.ppermute(value, BOTH, way)  271 us
    ppermute x76, starting transfers between devices, move(): return lax.ppermute(value, BOTH, way)  83.9 us
    psum x1, waiting for transfers between devices, local(): lax.psum(jnp.concatenate([head_grads.reshape(-1), table_grads.reshape(-1)...  63.1 us
    pallas_call x2, Pallas kernels, attention_backward(): pl.pallas_call(backward_kernel, grid_spec=pltpu.PrefetchScalarGridSpec(nu...  60.8 us
    unnamed x201, local copies, waits for them, and re-layouts  55.2 us
    unnamed x1, blocking collectives  45.4 us
    pallas_call x2, Pallas kernels, attention_forward(): pl.pallas_call(forward_kernel, grid_spec=pltpu.PrefetchScalarGridSpec(num...  38.4 us
    psum x1, blocking collectives, local(): act_grad = lax.psum(low(dot_nt(mod_grad, modulator)), 'mp').astype(F32)  38 us
  transfers between devices with their start and end apart: 79, of which 38 were waited for; matrix products, arithmetic and copies ran while one was open for 20% of the time, Pallas kernels for 4%

profile of v1, /device:TPU:0, one launch (start us, length us, event | category | flops | bytes accessed | tf_op | source)
XLA Modules:
  0.0 906.3 jit_solution(11049043470056475063)
XLA Ops:
  32.3 45.4 %all-reduce.2 = bf16[22288]{0:T(1024)(128)(2,1)S(1)} all-reduce(bf16[22288]{0:T(1024)(128)(2,1)S(1)} %dynamic-update-slice), channel_id=2, replica_groups=mesh['dp'=4,'mp'=8] {'mp'}, use_global_device_ids=true, to_apply=%add.2 | all-reduce | flops 22288 | bytes 89152
  121.5 9.4 %collective-permute-done.16 = bf16[144,1152]{1,0:T(8,128)(2,1)S(1)} collective-permute-done((bf16[144,1152]{1,0:T(8,128)(2,1)}, bf16[144,1152]{1,0:T(8,128)(2,1)S(1)}, u32[]{:S(2)}, u32[]{:S(2)}) %collective-permute-start.16) | collective-permute-done | bytes 331808 | tf_op jit(solution)/shard_map/ppermute | solution.py:55
  152.9 9.9 %collective-permute-done.19 = bf16[144,1152]{1,0:T(8,128)(2,1)S(1)} collective-permute-done((bf16[144,1152]{1,0:T(8,128)(2,1)}, bf16[144,1152]{1,0:T(8,128)(2,1)S(1)}, u32[]{:S(2)}, u32[]{:S(2)}) %collective-permute-start.19) | collective-permute-done | bytes 331808 | tf_op jit(solution)/shard_map/ppermute | solution.py:55
  189.7 11.3 %collective-permute-start.2 = (bf16[144,1152]{1,0:T(8,128)(2,1)}, bf16[144,1152]{1,0:T(8,128)(2,1)S(1)}, u32[]{:S(2)}, u32[]{:S(2)}) collective-permute-start(bf16[144,1152]{1,0:T(8,128)(2,1)} %collective-permute-done), channel_id=1, source_target_pairs={{0,2},{1,3},{2,4},{3,5},{4,6},{5,7},{6,0},{7,1},{8,10},{9,11},{10,... | collective-permute-start | bytes 995336 | tf_op jit(solution)/shard_map/ppermute | solution.py:55
  253.2 8.7 collective-permute-done.9
  296.6 10.5 %collective-permute-done.26 = bf16[144,1152]{1,0:T(8,128)(2,1)S(1)} collective-permute-done((bf16[144,1152]{1,0:T(8,128)(2,1)S(1)}, bf16[144,1152]{1,0:T(8,128)(2,1)S(1)}, u32[]{:S(2)}, u32[]{:S(2)}) %collective-permute-start.26) | collective-permute-done | bytes 331808 | tf_op jit(solution)/shard_map/ppermute | solution.py:55
  328.0 18.9 %shard_map.263 = (bf16[8,512,144]{2,1,0:T(8,128)(2,1)S(1)}, bf16[8,512,144]{2,1,0:T(8,128)(2,1)S(1)}, bf16[8,2,256,256]{3,2,1,0:T(8,128)(2,1)S(1)}, f32[512,1152]{1,0:T(8,128)S(1)}) custom-call(s32[1]{0:T(128)} %bitcast.2.half, bf16[512,1152]{1,0:T(8,128)(2,1)S(1)} %fusion.29.x_ref, bf16[8,2,144,1152]{3,2,1,0:T(8,128)(2,1)} %bitcast.11.w_ref, ...), custom_call_target="tpu_custom_call" | custom-call | flops 8757706752 | bytes 20971520 | tf_op jit(solution)/shard_map/pallas_call | solution.py:281
  350.9 19.5 %shard_map.264 = (bf16[8,512,144]{2,1,0:T(8,128)(2,1)S(1)}, bf16[8,512,144]{2,1,0:T(8,128)(2,1)S(1)}, bf16[8,2,256,256]{3,2,1,0:T(8,128)(2,1)S(1)}, f32[512,1152]{1,0:T(8,128)S(1)}) custom-call(s32[1]{0:T(128)} %bitcast.2.half, bf16[512,1152]{1,0:T(8,128)(2,1)S(1)} %fusion.29.x_ref, bf16[8,2,144,1152]{3,2,1,0:T(8,128)(2,1)} %bitcast.33.w_ref, ...), custom_call_target="tpu_custom_call" | custom-call | flops 8757706752 | bytes 20971520 | tf_op jit(solution)/shard_map/pallas_call | solution.py:281
  386.0 10.4 %convert_reduce_fusion = (f32[2304]{0:T(1024)S(1)}, bf16[512,2304]{1,0:T(8,128)(2,1)}) fusion(f32[512,2304]{1,0:T(8,128)S(1)} %convolution_add_fusion, bf16[512,1152]{1,0:T(8,128)(2,1)S(1)} %copy-done.34, bf16[2304,1152]{1,0:T(8,128)(2,1)} %collective-permute-done.44), kind=kOutput, calls=%fused_computation.26 | convolution fusion | flops 2743858944 | bytes 13575168 | tf_op jit(solution)/shard_map/dot_general | solution.py:155
  402.8 9.5 %convert_reduce_fusion.1 = (f32[2304]{0:T(1024)S(1)}, bf16[512,2304]{1,0:T(8,128)(2,1)S(1)}) fusion(f32[512,2304]{1,0:T(8,128)S(1)} %convolution_add_fusion.1, bf16[512,1152]{1,0:T(8,128)(2,1)S(1)} %copy-done.35, bf16[2304,1152]{1,0:T(8,128)(2,1)} %constant_dynamic-update-slice_fusion.31), kind=kOutput, calls=%fused_computation.27 | convolution fusion | flops 2743858944 | bytes 13575168 | tf_op jit(solution)/shard_map/dot_general | solution.py:155
  438.5 10.3 %convert_reduce_fusion.3 = (f32[1152]{0:T(1024)}, bf16[512,1152]{1,0:T(8,128)(2,1)S(1)}, f32[512,1152]{1,0:T(8,128)}, bf16[512,1152]{1,0:T(8,128)(2,1)}, f32[512,1152]{1,0:T(8,128)}) fusion(f32[2,1152]{1,0:T(2,128)S(1)} %bitcast.456, f32[512]{0:T(512)S(1)} %broadcast_multiply_fusion.2, f32[512]{0:T(512)S(1)} %add_rsqrt_fusion, ...), kind=kOutput, calls=%fused_computation.76 | convolution fusion | flops 2740321280 | bytes 25409536 | tf_op jit(solution)/shard_map/dot_general | solution.py:163
  448.9 30.4 %shard_map.266 = (bf16[8,2,144,1152]{3,2,1,0:T(8,128)(2,1)}, f32[8,2,144]{2,1,0:T(2,128)S(1)}, f32[8,16,512]{2,1,0:T(8,128)S(1)}, f32[512,1152]{1,0:T(8,128)}) custom-call(s32[1]{0:T(128)} %bitcast.2.half, bf16[512,1152]{1,0:T(8,128)(2,1)S(1)} %fusion.29.x_ref, bf16[512,1152]{1,0:T(8,128)(2,1)S(1)} %get-tuple-element.61.g_ref, ...), custom_call_target="tpu_custom_call" | custom-call | flops 20535312384 | bytes 31457280 | tf_op jit(solution)/shard_map/pallas_call | solution.py:318
  482.5 30.4 %shard_map.265 = (bf16[8,2,144,1152]{3,2,1,0:T(8,128)(2,1)}, f32[8,2,144]{2,1,0:T(2,128)S(1)}, f32[8,16,512]{2,1,0:T(8,128)S(1)}, f32[512,1152]{1,0:T(8,128)}) custom-call(s32[1]{0:T(128)} %bitcast.2.half, bf16[512,1152]{1,0:T(8,128)(2,1)S(1)} %fusion.29.x_ref, bf16[512,1152]{1,0:T(8,128)(2,1)S(1)} %get-tuple-element.61.g_ref, ...), custom_call_target="tpu_custom_call" | custom-call | flops 20535312384 | bytes 31457280 | tf_op jit(solution)/shard_map/pallas_call | solution.py:318
  539.2 8.8 convolution_convert_fusion
  554.7 38.0 %psum.14 = bf16[16,1152]{1,0:T(8,128)(2,1)S(1)} all-reduce(bf16[16,1152]{1,0:T(8,128)(2,1)S(1)} %convolution_convert_fusion.2), channel_id=1, replica_groups=mesh['dp'=4,'mp'=8] {'mp'}, use_global_device_ids=true, to_apply=%region_17.18 | all-reduce | flops 18432 | bytes 73728 | tf_op jit(solution)/shard_map/psum | solution.py:549
  607.9 63.1 %all-reduce.5.cloned.1.call-done = f32[24592]{0:T(1024)} async-done(((f32[24592]{0:T(1024)}), f32[24592]{0:T(1024)}) %all-reduce.5.cloned.1.call-update) | async-done | bytes 98384 | tf_op jit(solution)/shard_map/psum | solution.py:561
  699.4 7.8 add_convert_fusion
  721.1 8.5 collective-permute-done.62
  738.9 31.8 %collective-permute-done.46 = bf16[4,144,1152]{2,1,0:T(8,128)(2,1)S(1)} collective-permute-done((bf16[4,144,1152]{2,1,0:T(8,128)(2,1)S(1)}, bf16[4,144,1152]{2,1,0:T(8,128)(2,1)S(1)}, u32[]{:S(2)}, u32[]{:S(2)}) %collective-permute-start.46) | collective-permute-done | bytes 1327136 | tf_op jit(solution)/shard_map/ppermute | solution.py:55
  772.5 23.5 %collective-permute-done.66 = bf16[4,144,1152]{2,1,0:T(8,128)(2,1)S(1)} collective-permute-done((bf16[4,144,1152]{2,1,0:T(8,128)(2,1)S(1)}, bf16[4,144,1152]{2,1,0:T(8,128)(2,1)S(1)}, u32[]{:S(2)}, u32[]{:S(2)}) %collective-permute-start.66) | collective-permute-done | bytes 1327136 | tf_op jit(solution)/shard_map/ppermute | solution.py:55
  807.9 16.6 %collective-permute-done.67 = bf16[4,144,1152]{2,1,0:T(8,128)(2,1)S(1)} collective-permute-done((bf16[4,144,1152]{2,1,0:T(8,128)(2,1)S(1)}, bf16[4,144,1152]{2,1,0:T(8,128)(2,1)S(1)}, u32[]{:S(2)}, u32[]{:S(2)}) %collective-permute-start.67) | collective-permute-done | bytes 1327136 | tf_op jit(solution)/shard_map/ppermute | solution.py:55
  830.8 11.2 %collective-permute-done.69 = bf16[144,1152]{1,0:T(8,128)(2,1)S(1)} collective-permute-done((bf16[144,1152]{1,0:T(8,128)(2,1)S(1)}, bf16[144,1152]{1,0:T(8,128)(2,1)S(1)}, u32[]{:S(2)}, u32[]{:S(2)}) %collective-permute-start.69) | collective-permute-done | bytes 331808 | tf_op jit(solution)/shard_map/ppermute | solution.py:55
  868.2 13.7 %collective-permute-done.52 = bf16[2,144,1152]{2,1,0:T(8,128)(2,1)S(1)} collective-permute-done((bf16[2,144,1152]{2,1,0:T(8,128)(2,1)S(1)}, bf16[2,144,1152]{2,1,0:T(8,128)(2,1)S(1)}, u32[]{:S(2)}, u32[]{:S(2)}) %collective-permute-start.52) | collective-permute-done | bytes 663584 | tf_op jit(solution)/shard_map/ppermute | solution.py:55
  882.4 9.2 %collective-permute-done.74 = bf16[2,144,1152]{2,1,0:T(8,128)(2,1)S(1)} collective-permute-done((bf16[2,144,1152]{2,1,0:T(8,128)(2,1)S(1)}, bf16[2,144,1152]{2,1,0:T(8,128)(2,1)S(1)}, u32[]{:S(2)}, u32[]{:S(2)}) %collective-permute-start.74) | collective-permute-done | bytes 663584 | tf_op jit(solution)/shard_map/ppermute | solution.py:55
  (553 shorter events, 432.3 us)
Async XLA Ops:
  10.9 228.2 %collective-permute-start.6 = (bf16[144,1152]{1,0:T(8,128)(2,1)}, bf16[144,1152]{1,0:T(8,128)(2,1)}, u32[]{:S(2)}, u32[]{:S(2)}) collective-permute-start(bf16[144,1152]{1,0:T(8,128)(2,1)} %get-tuple-element.79), channel_id=1, source_target_pairs={{0,1},{1,0},{2,3},{3,2},{4,5},{5,4},{6,7},{7,6},{8,9},{9,8},{10,11... | collective-permute-start | bytes 995336 | tf_op jit(solution)/shard_map/ppermute | solution.py:55
  13.8 175.9 %collective-permute-start.4 = (bf16[144,1152]{1,0:T(8,128)(2,1)}, bf16[144,1152]{1,0:T(8,128)(2,1)}, u32[]{:S(2)}, u32[]{:S(2)}) collective-permute-start(bf16[144,1152]{1,0:T(8,128)(2,1)} %get-tuple-element.79), channel_id=1, source_target_pairs={{0,6},{1,7},{2,0},{3,1},{4,2},{5,3},{6,4},{7,5},{8,14},{9,15},{10,... | collective-permute-start | bytes 995336 | tf_op jit(solution)/shard_map/ppermute | solution.py:55
  17.4 100.5 %collective-permute-start = (bf16[144,1152]{1,0:T(8,128)(2,1)}, bf16[144,1152]{1,0:T(8,128)(2,1)}, u32[]{:S(2)}, u32[]{:S(2)}) collective-permute-start(bf16[144,1152]{1,0:T(8,128)(2,1)} %get-tuple-element.79), channel_id=1, source_target_pairs={{0,2},{1,3},{2,4},{3,5},{4,6},{5,7},{6,0},{7,1},{8,10},{9,11},{10,... | collective-permute-start | bytes 995336 | tf_op jit(solution)/shard_map/ppermute | solution.py:55
  18.8 302.0 %all-to-all-start = ((f32[8,2,864]{2,1,0:T(2,128)}), f32[8,2,864]{2,1,0:T(2,128)}, u32[]{:S(2)}, u32[]{:S(2)}) async-start(f32[8,2,864]{2,1,0:T(2,128)} %reshape.642), calls=%async_computation | async-start | bytes 114688 | tf_op jit(solution)/shard_map/all_to_all | solution.py:462
  25.6 113.0 %collective-permute-start.18 = (bf16[144,1152]{1,0:T(8,128)(2,1)}, bf16[144,1152]{1,0:T(8,128)(2,1)}, u32[]{:S(2)}, u32[]{:S(2)}) collective-permute-start(bf16[144,1152]{1,0:T(8,128)(2,1)} %get-tuple-element.69), channel_id=1, source_target_pairs={{0,6},{1,7},{2,0},{3,1},{4,2},{5,3},{6,4},{7,5},{8,14},{9,15},{10,... | collective-permute-start | bytes 995336 | tf_op jit(solution)/shard_map/ppermute | solution.py:55
  29.5 90.3 %collective-permute-start.15 = (bf16[144,1152]{1,0:T(8,128)(2,1)}, bf16[144,1152]{1,0:T(8,128)(2,1)}, u32[]{:S(2)}, u32[]{:S(2)}) collective-permute-start(bf16[144,1152]{1,0:T(8,128)(2,1)} %get-tuple-element.71), channel_id=1, source_target_pairs={{0,2},{1,3},{2,4},{3,5},{4,6},{5,7},{6,0},{7,1},{8,10},{9,11},{10,... | collective-permute-start | bytes 995336 | tf_op jit(solution)/shard_map/ppermute | solution.py:55
  162.8 39.0 %collective-permute-start.21 = (bf16[144,1152]{1,0:T(8,128)(2,1)}, bf16[144,1152]{1,0:T(8,128)(2,1)S(1)}, u32[]{:S(2)}, u32[]{:S(2)}) collective-permute-start(bf16[144,1152]{1,0:T(8,128)(2,1)} %get-tuple-element.71), channel_id=1, source_target_pairs={{0,1},{1,0},{2,3},{3,2},{4,5},{5,4},{6,7},{7,6},{8,9},{9,8},{10,11... | collective-permute-start | bytes 995336 | tf_op jit(solution)/shard_map/ppermute | solution.py:55
  201.1 73.0 %collective-permute-start.12 = (bf16[144,1152]{1,0:T(8,128)(2,1)}, bf16[144,1152]{1,0:T(8,128)(2,1)S(1)}, u32[]{:S(2)}, u32[]{:S(2)}) collective-permute-start(bf16[144,1152]{1,0:T(8,128)(2,1)} %collective-permute-done.4), channel_id=1, source_target_pairs={{0,1},{1,0},{2,3},{3,2},{4,5},{5,4},{6,7},{7,6},{8,9},{9,8},{10,11... | collective-permute-start | bytes 995336 | tf_op jit(solution)/shard_map/ppermute | solution.py:55
  235.1 46.7 %collective-permute-start.27 = (bf16[144,1152]{1,0:T(8,128)(2,1)S(1)}, bf16[144,1152]{1,0:T(8,128)(2,1)S(1)}, u32[]{:S(2)}, u32[]{:S(2)}) collective-permute-start(bf16[144,1152]{1,0:T(8,128)(2,1)S(1)} %collective-permute-done.20), channel_id=1, source_target_pairs={{0,1},{1,0},{2,3},{3,2},{4,5},{5,4},{6,7},{7,6},{8,9},{9,8},{10,11... | collective-permute-start | bytes 995336 | tf_op jit(solution)/shard_map/ppermute | solution.py:55
  239.1 43.4 %collective-permute-start.41 = (bf16[144,1152]{1,0:T(8,128)(2,1)S(1)}, bf16[144,1152]{1,0:T(8,128)(2,1)S(1)}, u32[]{:S(2)}, u32[]{:S(2)}) collective-permute-start(bf16[144,1152]{1,0:T(8,128)(2,1)S(1)} %collective-permute-done.34), channel_id=1, source_target_pairs={{0,1},{1,0},{2,3},{3,2},{4,5},{5,4},{6,7},{7,6},{8,9},{9,8},{10,11... | collective-permute-start | bytes 995336 | tf_op jit(solution)/shard_map/ppermute | solution.py:55
  292.3 58.6 %collective-permute-start.14 = (bf16[2304,1152]{1,0:T(8,128)(2,1)}, bf16[2304,1152]{1,0:T(8,128)(2,1)}, u32[]{:S(2)}, u32[]{:S(2)}) collective-permute-start(bf16[2304,1152]{1,0:T(8,128)(2,1)} %constant_dynamic-update-slice_fusion), channel_id=1, source_target_pairs={{0,8},{1,9},{2,10},{3,11},{4,12},{5,13},{6,14},{7,15},{8,0},{9,1},... | collective-permute-start | bytes 15925256 | tf_op jit(solution)/shard_map/ppermute | solution.py:55
  309.4 70.3 %collective-permute-start.43 = (bf16[2304,1152]{1,0:T(8,128)(2,1)}, bf16[2304,1152]{1,0:T(8,128)(2,1)}, u32[]{:S(2)}, u32[]{:S(2)}) collective-permute-start(bf16[2304,1152]{1,0:T(8,128)(2,1)} %constant_dynamic-update-slice_fusion.15), channel_id=1, source_target_pairs={{0,8},{1,9},{2,10},{3,11},{4,12},{5,13},{6,14},{7,15},{8,0},{9,1},... | collective-permute-start | bytes 15925256 | tf_op jit(solution)/shard_map/ppermute | solution.py:55
  314.6 71.4 %collective-permute-start.44 = (bf16[2304,1152]{1,0:T(8,128)(2,1)}, bf16[2304,1152]{1,0:T(8,128)(2,1)}, u32[]{:S(2)}, u32[]{:S(2)}) collective-permute-start(bf16[2304,1152]{1,0:T(8,128)(2,1)} %constant_dynamic-update-slice_fusion.31), channel_id=1, source_target_pairs={{0,8},{1,9},{2,10},{3,11},{4,12},{5,13},{6,14},{7,15},{8,0},{9,1},... | collective-permute-start | bytes 15925256 | tf_op jit(solution)/shard_map/ppermute | solution.py:55
  518.4 158.4 %collective-permute-start.54 = (bf16[2304,1152]{1,0:T(8,128)(2,1)}, bf16[2304,1152]{1,0:T(8,128)(2,1)}, u32[]{:S(2)}, u32[]{:S(2)}) collective-permute-start(bf16[2304,1152]{1,0:T(8,128)(2,1)} %convolution_convert_fusion.1), channel_id=1, source_target_pairs={{0,8},{1,9},{2,10},{3,11},{4,12},{5,13},{6,14},{7,15},{8,0},{9,1},... | collective-permute-start | bytes 15925256 | tf_op jit(solution)/shard_map/ppermute | solution.py:55
  525.6 145.4 %all-reduce.5.cloned.1.call-start = ((), (), s32[]{:S(2)}) async-start(), calls=%async_computation.2 | async-start | bytes 204800 | tf_op jit(solution)/shard_map/psum | solution.py:561
  537.5 152.9 %collective-permute-start.45 = (bf16[2304,1152]{1,0:T(8,128)(2,1)}, bf16[2304,1152]{1,0:T(8,128)(2,1)}, u32[]{:S(2)}, u32[]{:S(2)}) collective-permute-start(bf16[2304,1152]{1,0:T(8,128)(2,1)} %bitcast.470), channel_id=1, source_target_pairs={{0,8},{1,9},{2,10},{3,11},{4,12},{5,13},{6,14},{7,15},{8,0},{9,1},... | collective-permute-start | bytes 15925256 | tf_op jit(solution)/shard_map/ppermute | solution.py:55
  549.1 148.8 %collective-permute-start.65 = (bf16[2304,1152]{1,0:T(8,128)(2,1)}, bf16[2304,1152]{1,0:T(8,128)(2,1)}, u32[]{:S(2)}, u32[]{:S(2)}) collective-permute-start(bf16[2304,1152]{1,0:T(8,128)(2,1)} %convolution_convert_fusion), channel_id=1, source_target_pairs={{0,8},{1,9},{2,10},{3,11},{4,12},{5,13},{6,14},{7,15},{8,0},{9,1},... | collective-permute-start | bytes 15925256 | tf_op jit(solution)/shard_map/ppermute | solution.py:55
  688.8 41.0 %collective-permute-start.55 = (bf16[4,144,1152]{2,1,0:T(8,128)(2,1)S(1)}, bf16[4,144,1152]{2,1,0:T(8,128)(2,1)}, u32[]{:S(2)}, u32[]{:S(2)}) collective-permute-start(bf16[4,144,1152]{2,1,0:T(8,128)(2,1)S(1)} %slice_bitcast_fusion.3), channel_id=1, source_target_pairs={{0,16},{1,17},{2,18},{3,19},{4,20},{5,21},{6,22},{7,23},{8,24},{9,... | collective-permute-start | bytes 3981320 | tf_op jit(solution)/shard_map/ppermute | solution.py:55
  697.2 105.3 %collective-permute-start.48 = (bf16[3,144,1152]{2,1,0:T(8,128)(2,1)}, bf16[3,144,1152]{2,1,0:T(8,128)(2,1)}, u32[]{:S(2)}, u32[]{:S(2)}) collective-permute-start(bf16[3,144,1152]{2,1,0:T(8,128)(2,1)} %slice_bitcast_fusion.9), channel_id=1, source_target_pairs={{0,16},{1,17},{2,18},{3,19},{4,20},{5,21},{6,22},{7,23},{8,24},{9,... | collective-permute-start | bytes 2985992 | tf_op jit(solution)/shard_map/ppermute | solution.py:55
  697.9 72.8 %collective-permute-start.46 = (bf16[4,144,1152]{2,1,0:T(8,128)(2,1)S(1)}, bf16[4,144,1152]{2,1,0:T(8,128)(2,1)S(1)}, u32[]{:S(2)}, u32[]{:S(2)}) collective-permute-start(bf16[4,144,1152]{2,1,0:T(8,128)(2,1)S(1)} %slice_bitcast_fusion.6), channel_id=1, source_target_pairs={{0,16},{1,17},{2,18},{3,19},{4,20},{5,21},{6,22},{7,23},{8,24},{9,... | collective-permute-start | bytes 3981320 | tf_op jit(solution)/shard_map/ppermute | solution.py:55
  729.6 66.4 %collective-permute-start.66 = (bf16[4,144,1152]{2,1,0:T(8,128)(2,1)S(1)}, bf16[4,144,1152]{2,1,0:T(8,128)(2,1)S(1)}, u32[]{:S(2)}, u32[]{:S(2)}) collective-permute-start(bf16[4,144,1152]{2,1,0:T(8,128)(2,1)S(1)} %slice_bitcast_fusion), channel_id=1, source_target_pairs={{0,16},{1,17},{2,18},{3,19},{4,20},{5,21},{6,22},{7,23},{8,24},{9,... | collective-permute-start | bytes 3981320 | tf_op jit(solution)/shard_map/ppermute | solution.py:55
  734.6 63.3 %collective-permute-start.56 = (bf16[4,144,1152]{2,1,0:T(8,128)(2,1)S(1)}, bf16[4,144,1152]{2,1,0:T(8,128)(2,1)S(1)}, u32[]{:S(2)}, u32[]{:S(2)}) collective-permute-start(bf16[4,144,1152]{2,1,0:T(8,128)(2,1)S(1)} %fusion.22), channel_id=1, source_target_pairs={{0,1},{1,0},{2,3},{3,2},{4,5},{5,4},{6,7},{7,6},{8,9},{9,8},{10,11... | collective-permute-start | bytes 3981320 | tf_op jit(solution)/shard_map/ppermute | solution.py:55
  798.3 46.9 %collective-permute-start.57 = (bf16[144,1152]{1,0:T(8,128)(2,1)S(1)}, bf16[144,1152]{1,0:T(8,128)(2,1)S(1)}, u32[]{:S(2)}, u32[]{:S(2)}) collective-permute-start(bf16[144,1152]{1,0:T(8,128)(2,1)S(1)} %get-tuple-element.93), channel_id=1, source_target_pairs={{0,2},{1,3},{2,4},{3,5},{4,6},{5,7},{6,0},{7,1},{8,10},{9,11},{10,... | collective-permute-start | bytes 995336 | tf_op jit(solution)/shard_map/ppermute | solution.py:55
  804.0 47.9 %collective-permute-start.49 = (bf16[144,1152]{1,0:T(8,128)(2,1)S(1)}, bf16[144,1152]{1,0:T(8,128)(2,1)S(1)}, u32[]{:S(2)}, u32[]{:S(2)}) collective-permute-start(bf16[144,1152]{1,0:T(8,128)(2,1)S(1)} %get-tuple-element.95), channel_id=1, source_target_pairs={{0,2},{1,3},{2,4},{3,5},{4,6},{5,7},{6,0},{7,1},{8,10},{9,11},{10,... | collective-permute-start | bytes 995336 | tf_op jit(solution)/shard_map/ppermute | solution.py:55
  (125 other events, 1937.9 us)
Sparse Core Ops, SparseCore 0:
  549.2 121.7 all-reduce.4

commit v2 on v1

v2 whole, which is shorter than its diff:
```python
from functools import partial

import jax
import jax.numpy as jnp
from jax import lax
from jax.experimental import pallas as pl
from jax.experimental.pallas import tpu as pltpu
from jax.sharding import PartitionSpec as P

HS = 72
EPSILON = 1e-06
HIGHEST = lax.Precision.HIGHEST
BOTH = ("dp", "mp")
VMEM_BYTES = 44 * 2**20
BF16 = jnp.bfloat16
F32 = jnp.float32


def low(value):
    return value.astype(BF16)


def low_sum(*values):
    total = values[0].astype(F32)
    for value in values[1:]:
        total = total + value.astype(F32)
    return low(total)


def together(moved, held):
    return lax.optimization_barrier((moved, held))


class Step:
    def __init__(self, holder):
        self.holder = holder

    def __call__(self, moves, *names):
        moved = [lax.ppermute(value, BOTH, way) for value, way in moves]
        held = [getattr(self.holder, name) for name in names]
        moved, held = together(moved, held)
        for name, value in zip(names, held):
            setattr(self.holder, name, value)
        return moved


class GroupSum:
    def __init__(self):
        self.near_m, self.near_n, self.far_m, self.far_n = {}, {}, {}, {}

    def near(self, k, own, came):
        self.near_m[k], self.near_n[k] = [own[0], came[0]], [own[1], came[1]]

    def far(self, k, own, came):
        self.far_m[k], self.far_n[k] = [own[0], came[0]], [own[1], came[1]]

    def send(self, *terms):
        return jnp.stack([low_sum(*term) for term in terms])

    def done_pair(self):
        self.kept = self.send(self.near_n[0], self.near_m[0])
        return self.kept

    def done(self, crossed):
        return low_sum(self.kept[::-1], crossed)


class PairPlan:
    chunks = (((0, 0), (0, 1)), ((1, 0), (3, 0)), ((1, 1), (3, 1)), ((2, 0), (2, 1)))

    def __init__(self, mesh):
        self.zs = mesh.shape["mp"] // 2
        zs = self.zs
        self.core = self.moves(lambda y, c, z, x: (y, 1 - c, z, x))
        self.across_x = self.moves(lambda y, c, z, x: (y, c, z, 1 - x))
        self.across_y = self.moves(lambda y, c, z, x: (1 - y, c, z, x))
        self.up = self.moves(lambda y, c, z, x: (y, c, (z + 1) % zs, x))
        self.down = self.moves(lambda y, c, z, x: (y, c, (z - 1) % zs, x))

    def moves(self, target):
        def number(y, c, z, x):
            return ((y * 2 + c) * self.zs + z) * 2 + x

        places = [(y, c, z, x) for y in (0, 1) for c in (0, 1) for z in range(self.zs) for x in (0, 1)]
        return [(number(*place), number(*target(*place))) for place in places]

    def here(self):
        dp, mp = lax.axis_index("dp"), lax.axis_index("mp")
        return dp // 2, dp % 2, mp // 2, mp % 2

    def first_half(self):
        return self.here()[0]

    def turned(self, values, halves):
        y, c, z, x = self.here()
        places = jnp.arange(self.zs)
        pick = (places[:, None] + places[None, :]) % self.zs == z
        pick = pick.reshape(pick.shape + (1,) * (values.ndim - 1))
        values = jnp.sum(jnp.where(pick, values[None], jnp.zeros_like(values[None])), axis=1)
        values = jnp.where(x == 0, values, values[:, ::-1])
        values = jnp.where(c == 0, values, values[:, :, ::-1])
        if halves:
            values = jnp.where(y == 0, values, values[:, :, :, ::-1])
        return values

    def to_own(self, values):
        rest = values.shape[1:]
        split = self.turned(values.reshape((self.zs, 2, 2) + rest), False)
        split = split.transpose((2, 0, 1) + tuple(range(3, split.ndim)))
        return split.reshape((2, values.shape[0] // 2) + rest)

    def to_whole(self, values):
        rest = values.shape[2:]
        split = values.reshape((2, self.zs, 2) + rest)
        split = split.transpose((1, 2, 0) + tuple(range(3, split.ndim)))
        return self.turned(split, False).reshape((-1,) + rest)

    def units_to_whole(self, values):
        split = self.turned(values.reshape(self.zs, 2, 2, 2, -1), True)
        return split.transpose(0, 1, 3, 2, 4).reshape(-1)

    def unit_order(self):
        y, c, z, x = self.here()
        shards = [((z - k) % self.zs) * 2 + (x ^ j) for k in range(self.zs) for j in range(2)]
        quarters = [(y ^ half) * 2 + (c ^ core) for core in range(2) for half in range(2)]
        return jnp.stack(shards).astype(jnp.int32), jnp.stack(quarters).astype(jnp.int32)

    def chunk(self, number, values):
        return jnp.stack([values[2 * k + j] for k, j in self.chunks[number]])

    def in_slots(self, parts):
        slots = {}
        for number, part in enumerate(parts):
            for place, (k, j) in enumerate(self.chunks[number]):
                slots[2 * k + j] = part[place]
        return jnp.stack([slots[place] for place in range(len(slots))])

    def pieces(self, shard, core_first):
        y, c, _, _ = self.here()
        rows, width = shard.shape
        split = shard.reshape(2, 2, rows // 4, width)
        mine = lax.dynamic_index_in_dim(split, c, 0 if core_first else 1, keepdims=False)
        return jnp.where(y == 0, mine, mine[::-1])

    def whole_shard(self, mine, others, core_first):
        y, c, _, _ = self.here()
        both = jnp.stack([mine, others])
        both = jnp.where(y == 0, both, both[:, ::-1])
        both = jnp.where(c == 0, both, both[::-1])
        both = both if core_first else both.transpose(1, 0, 2, 3)
        return both.reshape(-1, both.shape[-1]).astype(F32)

    def sum_groups(self, value):
        value = value + lax.ppermute(value, BOTH, self.core)
        return value + lax.ppermute(value, BOTH, self.across_y)

    def gather_groups(self, value):
        y, c, _, _ = self.here()
        other = lax.ppermute(value, BOTH, self.core)
        both = jnp.where(c == 0, jnp.stack([value, other]), jnp.stack([other, value]))
        other = lax.ppermute(both, BOTH, self.across_y)
        both = jnp.where(y == 0, jnp.stack([both, other]), jnp.stack([other, both]))
        return both.reshape((-1,) + value.shape[1:])

    def run(self, work):
        step = Step(work)
        up, down, x, y, core = self.up, self.down, self.across_x, self.across_y, self.core
        stack = lambda *values: jnp.stack(values)
        attn = self.pieces(work.attn_rows, True)
        feed = self.pieces(work.down_rows, False)
        quarters = work.up_rows.reshape(4, -1, work.width)
        work.quarter = lax.dynamic_index_in_dim(quarters, lax.axis_index("dp"), 0, keepdims=False)

        work.modulate()
        a1, a3, f0 = step(
            [(attn[0], up), (attn[0], down), (attn, x)], "modulation", "tokens", "small", "offset_index", "quarter"
        )
        work.norm_one()
        work.gather_small()
        own = stack(attn, f0)
        a2, n1, xm3, other, d1 = step(
            [(a1, up), (a1, y), (a3, x), (own, core), (feed, up)], "input_one", "gathered_small", "quarter"
        )
        work.up_w = lax.all_gather(work.quarter, ("mp", "dp"), axis=0, tiled=True)
        work.forward_weights(0, own, other)
        work.prepare()
        near1 = stack(a1, n1)
        far1, came3, d3 = step([(near1, x), (stack(a3, xm3), y), (feed, down)], "windows", "input_one")
        near3, far3 = stack(a3, came3[0]), stack(xm3, came3[1])
        work.forward(0)
        own1, own2 = stack(near1, near3), stack(far1, far3)
        (xm2, dx0), dm2, dn2, other1, other2 = step(
            [(stack(a2, feed[0]), x), (d1[0], up), (d3[1], down), (own1, core), (own2, core)],
            "branch",
            "input_one",
        )
        work.forward_weights(1, own1, other1)
        work.forward_weights(2, own2, other2)
        work.forward(1)
        (n2, xn2, dy0), (dx1, dx3) = step(
            [(stack(a2, xm2, dx0), y), (stack(d1[0], d3[0]), x)], "branch", "input_one"
        )
        own3 = stack(stack(a2, n2), stack(xm2, xn2))
        work.forward(2)
        other3, dx2, (dy1, dy3) = step(
            [(own3, core), (dm2, x), (stack(dx1, dx3), y)], "branch", "input_one"
        )
        work.forward_weights(3, own3, other3)
        work.forward(3)
        down_own = [stack(feed, stack(dx0, dy0), d1, stack(dx1, dy1))]
        dy2, other_down = step([(dx2, y), (down_own[0], core)], "branch", "up_w")
        down_other = [other_down]
        work.norm_two()
        down_own.append(stack(stack(dm2, dn2), stack(dx2, dy2), d3, stack(dx3, dy3)))
        (other_down,) = step([(down_own[1], core)], "input_two", "mlp_grad")
        down_other.append(other_down)
        work.down_w = list(zip(down_own, down_other))
        work.units_forward()
        step([], "hidden", "slope", "down_grad", "units_in")

        work.down_part = lax.psum_scatter(
            work.down_grad.reshape(-1, work.width), ("mp", "dp"), scatter_dimension=0, tiled=True
        )
        units, heads = GroupSum(), GroupSum()

        def add_units(part, came):
            for k in (0, 1):
                own = work.up_grads[part][0]
                units.near(2 * part + k, own[2 * k], came[2 * k])
                units.far(2 * part + k, own[2 * k + 1], came[2 * k + 1])

        def add_heads(number, came):
            own = work.head_grads[number][0]
            for place, (k, j) in enumerate(self.chunks[number]):
                (heads.far if j else heads.near)(k, own[place], came[place])

        work.units_backward(0)
        step([], "up_grads", "units_in")
        work.units_backward(1)
        (came,) = step([(work.up_grads[0][1], core)], "up_grads", "grad_input_two_parts")
        add_units(0, came)
        work.norm_two_back()
        far0, got1, n1, came = step(
            [
                (units.send(units.far_m[0], units.far_n[0]), x),
                (units.send(units.far_n[1]), y),
                (units.send(units.near_n[1]), down),
                (work.up_grads[1][1], core),
            ],
            "attn_grad",
        )
        add_units(1, came)
        units.near_m[0].append(far0[0])
        units.near_n[0] += [far0[1], n1[0]]
        units.far_m[1].append(got1[0])
        work.backward(3)
        far1, got23, n2 = step(
            [
                (units.send(units.far_m[1]), x),
                (units.send(units.far_n[2], units.far_n[3]), y),
                (units.send(units.near_n[2]), up),
            ],
            "attn_grad",
            "head_grads",
        )
        units.near_m[1].append(far1[0])
        for place, k in enumerate((2, 3)):
            units.far_m[k].append(got23[place])
        units.near_n[3].append(n2[0])
        work.backward(2)
        far23, n3, came = step(
            [
                (units.send(units.far_m[2], units.far_m[3]), x),
                (units.send(units.near_n[3]), up),
                (work.head_grads[3][1], core),
            ],
            "attn_grad",
            "head_grads",
        )
        for place, k in enumerate((2, 3)):
            units.near_m[k].append(far23[place])
        units.near_n[0].append(n3[0])
        add_heads(3, came)
        work.backward(1)
        m2, m3, got2, came = step(
            [
                (units.send(units.near_m[2]), down),
                (units.send(units.near_m[3]), up),
                (heads.send(heads.far_n[2], heads.near_n[2]), y),
                (work.head_grads[2][1], core),
            ],
            "attn_grad",
            "head_grads",
        )
        units.near_m[1].append(m2[0])
        units.near_m[0].append(m3[0])
        heads.far_m[2].append(got2[0])
        heads.near_m[2].append(got2[1])
        add_heads(2, came)
        work.backward(0)
        m1, far2, got13, came = step(
            [
                (units.send(units.near_m[1]), down),
                (heads.send(heads.far_m[2]), x),
                (heads.send(heads.far_n[1], heads.far_n[3]), y),
                (work.head_grads[1][1], core),
            ],
            "hidden",
            "head_grads",
            "rows_grads",
            "down_part",
        )
        units.near_m[0].append(m1[0])
        heads.near_m[2].append(far2[0])
        for place, k in enumerate((1, 3)):
            heads.far_m[k].append(got13[place])
        add_heads(1, came)
        work.units_out()
        far13, got13, m2, came = step(
            [
                (heads.send(heads.far_m[1], heads.far_m[3]), x),
                (heads.send(heads.near_n[1], heads.near_n[3]), y),
                (heads.send(heads.near_m[2]), down),
                (work.head_grads[0][1], core),
            ],
            "mlp_parts",
            "rows_grads",
        )
        for place, k in enumerate((1, 3)):
            heads.near_m[k] += [far13[place], got13[place]]
        heads.near_m[1].append(m2[0])
        add_heads(0, came)
        work.finish_rows()
        far0, crossed, m3, m1 = step(
            [
                (heads.send(heads.far_m[0], heads.far_n[0]), x),
                (units.done_pair(), y),
                (heads.send(heads.near_m[3]), up),
                (heads.send(heads.near_m[1]), down),
            ],
            "sums",
            "mod_grad",
            "tokens_grad",
            "block_out",
        )
        heads.near_m[0] += [far0[0], m3[0], m1[0]]
        heads.near_n[0].append(far0[1])
        up_mine = units.done(crossed)
        work.finish_small()
        crossed, up_other = step([(heads.done_pair(), y), (up_mine, core)])
        attn_mine = heads.done(crossed)
        (attn_other,) = step([(attn_mine, core)])
        work.up_shard = self.whole_shard(up_mine, up_other, False)
        work.attn_shard = self.whole_shard(attn_mine, attn_other, True)
        work.down_shard = lax.all_gather(work.down_part, "dp", axis=0, tiled=True).astype(F32)


class PlainPlan:
    def __init__(self, mesh):
        self.shards = mesh.shape["mp"]

    def first_half(self):
        return jnp.int32(0)

    def to_own(self, values):
        return values.reshape((2, -1) + values.shape[1:])

    def to_whole(self, values):
        return values.reshape((-1,) + values.shape[2:])

    def units_to_whole(self, values):
        return values.reshape(-1)

    def unit_order(self):
        return jnp.arange(self.shards, dtype=jnp.int32), jnp.arange(4, dtype=jnp.int32)

    def chunk(self, number, values):
        return values

    def in_slots(self, parts):
        return parts[0]

    def sum_groups(self, value):
        return lax.psum(value, "dp")

    def gather_groups(self, value):
        return lax.all_gather(value, "dp", axis=0, tiled=True)

    def gather(self, shard):
        return lax.all_gather(shard, "mp", axis=0, tiled=True)

    def scatter(self, full):
        full = full.reshape(-1, full.shape[-1])
        part = lax.psum_scatter(full, "mp", scatter_dimension=0, tiled=True)
        return lax.psum(part, "dp").astype(F32)

    def run(self, work):
        work.modulate()
        work.norm_one()
        work.gather_small()
        work.prepare()
        attn = self.gather(work.attn_rows).reshape(2, -1, 2, 2 * HS, work.width)
        work.forward_weights(0, attn[0], attn[1])
        work.forward(0)
        work.norm_two()
        work.up_w = self.gather(work.up_rows)
        feed = self.gather(work.down_rows)
        feed = feed.reshape(2, self.shards // 2, 2, 2, -1, work.width)
        work.down_w = [(part[:, 0], part[:, 1]) for part in feed]
        work.units_forward()
        work.down_shard = self.scatter(work.down_grad)
        for part in (0, 1):
            work.units_backward(part)
        work.norm_two_back()
        up_grads = [jnp.stack(pair, axis=1) for pair in work.up_grads]
        work.up_shard = self.scatter(jnp.concatenate(up_grads))
        work.backward(0)
        work.attn_shard = self.scatter(jnp.stack(work.head_grads[0]))
        work.units_out()
        work.finish_rows()
        work.finish_small()


def dot_nt(left, right):
    return lax.dot_general(left, right, (((1,), (1,)), ((), ())), preferred_element_type=F32)


def dot_tn(left, right):
    return lax.dot_general(left, right, (((0,), (0,)), ((), ())), preferred_element_type=F32)


def dot_nn(left, right):
    return lax.dot_general(left, right, (((1,), (0,)), ((), ())), preferred_element_type=F32)


def forward_head(half, x_ref, w_ref, b_ref, window_ref, qk_ref, va_ref, soft_ref):
    first = half[0]
    samples, patches = soft_ref.shape[1], soft_ref.shape[2]
    grid_side = window_ref.shape[1]
    x = x_ref[...]
    w_qk = w_ref[0, first]
    w_vo = w_ref[0, 1 - first]
    qk = low(dot_nt(x, w_qk) + b_ref[0, 0:1])
    vo = low(dot_nt(x, w_vo) + b_ref[0, 1:2])
    qk_ref[0] = qk
    queries, keys, values = qk[:, :HS], qk[:, HS:], vo[:, :HS]
    window = window_ref[0]
    width = window.shape[1]
    bias = jnp.concatenate(
        [
            pltpu.roll(window, (width - (grid_side - 1 - row) * grid_side) % width, 1)[:, :patches]
            for row in range(grid_side)
        ],
        axis=0,
    )
    joined = []
    for sample in range(samples):
        rows = slice(sample * patches, (sample + 1) * patches)
        scores = dot_nt(queries[rows], keys[rows]) * HS ** (-0.5) + bias
        powers = jnp.exp(scores - jnp.max(scores, axis=-1, keepdims=True))
        soft = low(powers * (1.0 / jnp.sum(powers, axis=-1, keepdims=True)))
        soft_ref[0, sample] = soft
        attended = low(dot_nn(soft, values[rows]))
        joined.append(jnp.concatenate([values[rows], attended], axis=1))
    joined = jnp.concatenate(joined, axis=0)
    va_ref[0] = joined
    lane = lax.broadcasted_iota(jnp.int32, joined.shape, 1)
    return dot_nn(jnp.where(lane < HS, jnp.zeros_like(joined), joined), w_vo)


def add_up(sum_ref, part):
    @pl.when(pl.program_id(0) == 0)
    def _():
        sum_ref[...] = part

    @pl.when(pl.program_id(0) > 0)
    def _():
        sum_ref[...] += part


def forward_kernel(half, x_ref, *refs):
    ins, outs, sum_ref = refs[:6], refs[6:12], refs[12]
    part = forward_head(half, x_ref, *ins[:3], *outs[:3])
    part += forward_head(half, x_ref, *ins[3:], *outs[3:])
    add_up(sum_ref, part)


def backward_head(
    half, x_ref, g_ref, w_ref, qk_ref, va_ref, soft_ref, dw_ref, db_ref, dwindow_ref
):
    first = half[0]
    samples, patches = soft_ref.shape[1], soft_ref.shape[2]
    grid_side = dwindow_ref.shape[1]
    x = x_ref[...]
    grad = g_ref[...]
    w_qk = w_ref[0, first]
    w_vo = w_ref[0, 1 - first]
    grad_attended = low(dot_nt(grad, w_vo))[:, HS:]
    qk = qk_ref[0]
    va = va_ref[0]
    queries, keys, values = qk[:, :HS], qk[:, HS:], va[:, :HS]
    score_sum = None
    grads_qk, grads_v = [], []
    for sample in range(samples):
        rows = slice(sample * patches, (sample + 1) * patches)
        soft = soft_ref[0, sample]
        grad_here = grad_attended[rows]
        grad_soft = dot_nt(grad_here, values[rows])
        grads_v.append(dot_tn(soft, grad_here))
        weighted = soft.astype(F32) * grad_soft
        grad_scores = weighted - soft.astype(F32) * jnp.sum(weighted, axis=-1, keepdims=True)
        grad_scores = low(grad_scores)
        wide = grad_scores.astype(F32)
        score_sum = wide if score_sum is None else score_sum + wide
        grad_q = dot_nn(grad_scores, keys[rows]) * HS ** (-0.5)
        grad_k = dot_tn(grad_scores, queries[rows]) * HS ** (-0.5)
        grads_qk.append(jnp.concatenate([grad_q, grad_k], axis=1))
    grad_qk = low(jnp.concatenate(grads_qk, axis=0))
    grad_v = low(jnp.concatenate(grads_v, axis=0))
    grad_vo = jnp.concatenate([grad_v, jnp.zeros_like(grad_v)], axis=1)
    dw_qk = low(dot_tn(grad_qk, x))
    dw_vo = low(jnp.concatenate([dot_tn(grad_v, x), dot_tn(va[:, HS:], grad)], axis=0))
    dw_ref[0, 0] = lax.select(first == 0, dw_qk, dw_vo)
    dw_ref[0, 1] = lax.select(first == 0, dw_vo, dw_qk)
    db_ref[0, 0:1] = jnp.sum(grad_qk.astype(F32), axis=0, keepdims=True)
    db_ref[0, 1:2] = jnp.sum(grad_vo.astype(F32), axis=0, keepdims=True)
    width = dwindow_ref.shape[2]
    window = jnp.zeros((grid_side, width), F32)
    blank = jnp.zeros((grid_side, width - patches), F32)
    for row in range(grid_side):
        band = score_sum[row * grid_side : (row + 1) * grid_side]
        window = window + pltpu.roll(
            jnp.concatenate([band, blank], axis=1), (grid_side - 1 - row) * grid_side, 1
        )
    dwindow_ref[0] = window
    return dot_nn(grad_qk, w_qk) + dot_nn(grad_vo, w_vo)


def backward_kernel(half, x_ref, g_ref, *refs):
    ins, outs, sum_ref = refs[:8], refs[8:14], refs[14]
    part = backward_head(half, x_ref, g_ref, *ins[:4], *outs[:3])
    part += backward_head(half, x_ref, g_ref, *ins[4:], *outs[3:])
    add_up(sum_ref, part)


def same(shape):
    return pl.BlockSpec(shape, lambda head, half: (0,) * len(shape))


def per_head(shape):
    return pl.BlockSpec((1,) + shape, lambda head, half: (head,) + (0,) * len(shape))


def attention_forward(half, rows_in, weights, bias, windows, patches):
    heads = weights[0].shape[0]
    count, width = rows_in.shape
    samples = count // patches
    flops = heads * 4 * count * (width * 6 * HS + patches * 2 * HS)
    shapes = ((count, 2 * HS), (count, 2 * HS), (samples, patches, patches))
    *saved, branch = pl.pallas_call(
        forward_kernel,
        grid_spec=pltpu.PrefetchScalarGridSpec(
            num_scalar_prefetch=1,
            grid=(heads,),
            in_specs=[same(rows_in.shape)]
            + [per_head(value[0].shape[1:]) for value in (weights, bias, windows)] * 2,
            out_specs=[per_head(shape) for shape in shapes] * 2 + [same(rows_in.shape)],
        ),
        out_shape=[jax.ShapeDtypeStruct((heads,) + shape, BF16) for shape in shapes] * 2
        + [jax.ShapeDtypeStruct((count, width), F32)],
        compiler_params=pltpu.CompilerParams(vmem_limit_bytes=VMEM_BYTES),
        cost_estimate=pl.CostEstimate(
            flops=2 * flops, bytes_accessed=heads * 6 * 2**20, transcendentals=2 * heads * count * patches
        ),
    )(half, rows_in, *[value[part] for part in (0, 1) for value in (weights, bias, windows)])
    return (saved[:3], saved[3:]), branch


def attention_backward(half, rows_in, grad, weights, saved, window_shape, patches):
    heads = weights[0].shape[0]
    count, width = rows_in.shape
    samples = count // patches
    flops = heads * 4 * count * (width * 14 * HS + patches * 5 * HS)
    shapes = ((count, 2 * HS), (count, 2 * HS), (samples, patches, patches))
    results = ((weights[0].shape[1:], BF16), ((2, 2 * HS), F32), (window_shape, F32))
    *out, rows_grad = pl.pallas_call(
        backward_kernel,
        grid_spec=pltpu.PrefetchScalarGridSpec(
            num_scalar_prefetch=1,
            grid=(heads,),
            in_specs=[same(rows_in.shape), same(grad.shape)]
            + [per_head(shape) for shape in (weights[0].shape[1:],) + shapes] * 2,
            out_specs=[per_head(shape) for shape, _ in results] * 2 + [same(rows_in.shape)],
        ),
        out_shape=[jax.ShapeDtypeStruct((heads,) + shape, kind) for shape, kind in results] * 2
        + [jax.ShapeDtypeStruct((count, width), F32)],
        compiler_params=pltpu.CompilerParams(vmem_limit_bytes=VMEM_BYTES),
        cost_estimate=pl.CostEstimate(
            flops=2 * flops, bytes_accessed=heads * 10 * 2**20, transcendentals=0
        ),
    )(half, rows_in, grad, *[value for part in (0, 1) for value in (weights[part], *saved[part])])
    return (out[:3], out[3:]), rows_grad


def in_order(order, ref):
    return jnp.concatenate([ref[0, order[pl.num_programs(0) + part]] for part in range(4)], axis=0)


def units_forward_kernel(x_ref, g_ref, up_ref, b_ref, hidden_ref, slope_ref, grad_ref):
    weights = up_ref[0].reshape(-1, up_ref.shape[-1])
    value = dot_nt(weights, x_ref[...]) + b_ref[0]
    root, cubic = 0.7978845608028654, 0.044715
    square = value * value
    bent = jnp.tanh(root * value * (1.0 + cubic * square))
    above = 0.5 * (1.0 + bent)
    hidden = low(value * above)
    hidden_ref[0] = hidden.reshape(hidden_ref.shape[1:])
    slope = above + 0.5 * value * (1.0 - bent * bent) * (root * (1.0 + 3.0 * cubic * square))
    slope_ref[0] = low(slope).reshape(slope_ref.shape[1:])
    grad_ref[0] = low(dot_nn(hidden, g_ref[...])).reshape(grad_ref.shape[1:])


def units_backward_kernel(
    order, x_ref, g_ref, up_ref, slope_ref, down_ref, down_other_ref, own_ref, other_ref, b_ref, sum_ref
):
    width = x_ref.shape[1]
    down = jnp.concatenate([ref[0].reshape(-1, width) for ref in (down_ref, down_other_ref)], axis=0)
    grad_pre = low(dot_nt(down, g_ref[...]) * in_order(order, slope_ref).astype(F32))
    b_ref[0] = jnp.sum(grad_pre.astype(F32), axis=1, keepdims=True)
    grad = low(dot_nn(grad_pre, x_ref[...]))
    half = grad.shape[0] // 2
    own_ref[0] = grad[:half].reshape(own_ref.shape[1:])
    other_ref[0] = grad[half:].reshape(own_ref.shape[1:])
    add_up(sum_ref, dot_tn(grad_pre, in_order(order, up_ref)))


def units_out_kernel(order, hidden_ref, down_ref, down_other_ref, sum_ref):
    width = down_ref.shape[-1]
    down = jnp.concatenate([ref[0].reshape(-1, width) for ref in (down_ref, down_other_ref)], axis=0)
    add_up(sum_ref, dot_tn(in_order(order, hidden_ref), down))


def whole(shape):
    return pl.BlockSpec(shape, lambda slot, *order: (0,) * len(shape))


def by_slot(shape):
    return pl.BlockSpec((1,) + shape, lambda slot, *order: (slot,) + (0,) * len(shape))


def by_shard(shape):
    return pl.BlockSpec((1,) + shape, lambda slot, order: (order[slot],) + (0,) * len(shape))


def units_call(kernel, order, slots, inputs, outputs):
    return pl.pallas_call(
        kernel,
        grid_spec=pltpu.PrefetchScalarGridSpec(
            num_scalar_prefetch=len(order),
            grid=(slots,),
            in_specs=[
                kind(value.shape if kind is whole else value.shape[1:]) for kind, value in inputs
            ],
            out_specs=[kind(shape if kind is whole else shape[1:]) for kind, shape, _ in outputs],
        ),
        out_shape=[jax.ShapeDtypeStruct(shape, kept) for _, shape, kept in outputs],
        compiler_params=pltpu.CompilerParams(vmem_limit_bytes=VMEM_BYTES),
        cost_estimate=pl.CostEstimate(
            flops=slots * 4 * 10**8, bytes_accessed=slots * 8 * 2**20, transcendentals=0
        ),
    )(*order, *[value for _, value in inputs])


def window_entries(offset_index):
    side = int(round(offset_index.shape[0] ** 0.5))
    by_place = offset_index.reshape(side, side, side, side)
    rising = by_place[::-1, :, 0, :].transpose(1, 0, 2)
    unused = jnp.full((side, 1, side), -1, offset_index.dtype)
    return jnp.concatenate([rising, by_place[0, :, 1:, :], unused], axis=1)


def windows_kernel(entries_ref, table_ref, out_ref):
    wanted = entries_ref[0]
    place = lax.broadcasted_iota(jnp.int32, (table_ref.shape[1], wanted.shape[1]), 0)
    out_ref[0] = dot_nn(table_ref[...], low(jnp.where(place == wanted, 1.0, 0.0)))


def table_windows(table, entries):
    side = entries.shape[0]
    flat = entries.reshape(side, 1, -1)
    shape = (side, table.shape[0], flat.shape[2])
    (found,) = units_call(
        windows_kernel, (), side, [(by_slot, flat), (whole, table)], [(by_slot, shape, F32)]
    )
    return found.transpose(1, 0, 2)


def table_kernel(entries_ref, windows_ref, sum_ref):
    wanted = entries_ref[0]
    place = lax.broadcasted_iota(jnp.int32, (sum_ref.shape[1], wanted.shape[1]), 0)
    pick = low(jnp.where(place == wanted, 1.0, 0.0))
    rest = windows_ref[0]
    total = jnp.zeros(sum_ref.shape, F32)
    for _ in range(3):
        part = low(rest)
        total += dot_nt(part, pick)
        rest = rest - part.astype(F32)
    add_up(sum_ref, total)


def table_from_windows(windows, entries, table_rows):
    side = entries.shape[0]
    flat = entries.reshape(side, 1, -1)
    (total,) = units_call(
        table_kernel,
        (),
        side,
        [(by_slot, flat), (by_slot, windows.transpose(1, 0, 2))],
        [(whole, (windows.shape[0], table_rows), F32)],
    )
    return total


def normalize(values):
    centred = values - jnp.mean(values, axis=-1, keepdims=True)
    inverse = lax.rsqrt(jnp.mean(centred * centred, axis=-1, keepdims=True) + EPSILON)
    return (centred * inverse, inverse)


def norm_back(grad_normed, normed, inverse):
    first_mean = jnp.mean(grad_normed, axis=-1, keepdims=True)
    second_mean = jnp.mean(grad_normed * normed, axis=-1, keepdims=True)
    return (grad_normed - first_mean - normed * second_mean) * inverse


def attention_rows(qkv_weight, out_weight):
    width, _, local_width = qkv_weight.shape
    heads = local_width // HS
    qkv = qkv_weight.reshape(width, 3, heads, HS).transpose(2, 1, 3, 0)
    out = out_weight.reshape(heads, 1, HS, width)
    return jnp.concatenate([qkv, out], axis=1).reshape(heads * 4 * HS, width)


class Work:
    def __init__(
        self,
        plan,
        tokens,
        conditioning,
        counts,
        offset_index,
        modulator,
        modulator_bias,
        qkv_weight,
        qv_bias,
        offset_table,
        out_weight,
        out_bias,
        up_weight,
        up_bias,
        down_weight,
        down_bias,
        out_grad,
    ):
        self.plan = plan
        self.rows, self.width = tokens.shape
        self.patches = offset_index.shape[0]
        self.samples = self.rows // self.patches
        self.group_samples = conditioning.shape[0]
        self.shards = self.group_samples // self.samples
        self.columns = modulator.shape[1]
        self.local_width = qkv_weight.shape[2]
        self.local_heads = self.local_width // HS
        self.heads = self.local_heads * self.shards
        self.table_rows = offset_table.shape[0]
        self.local_units = up_weight.shape[1]
        self.by_sample = (self.samples, self.patches, self.width)
        self.flat = (self.rows, self.width)
        self.counts, self.offset_index = counts, offset_index
        self.tokens, self.out_grad = tokens, out_grad
        self.conditioning = conditioning.astype(F32)
        self.modulator, self.modulator_bias = modulator, modulator_bias
        self.out_bias, self.down_bias = out_bias, down_bias
        self.attn_rows = attention_rows(qkv_weight, out_weight)
        self.up_rows, self.down_rows = up_weight.T, down_weight
        self.small = jnp.concatenate([qv_bias.reshape(-1), offset_table.T.reshape(-1), up_bias])
        self.half = plan.first_half().reshape(1)
        self.order = plan.unit_order()
        self.attn_w, self.saved = {}, {}
        self.branch = []
        self.up_grads, self.unit_sums, self.grad_input_two_parts = [], [], []
        self.head_grads, self.head_extras, self.rows_grads = {}, {}, []
        self.mlp_parts = []

    def exchange(self, values):
        return lax.all_to_all(values, "mp", 0, 0)

    def to_all(self, values):
        return self.exchange(jnp.broadcast_to(values[None], (self.shards,) + values.shape))

    def modulate(self):
        self.activated = low(jax.nn.silu(self.conditioning))
        part = jnp.dot(self.activated, self.modulator, preferred_element_type=F32)
        part = part + self.modulator_bias.astype(F32)
        mod = self.exchange(part.reshape(self.shards, self.samples, self.columns))
        mod = mod.transpose(1, 0, 2).reshape(self.samples, 6, 1, self.width)
        self.modulation = [mod[:, number] for number in range(6)]

    def norm_one(self):
        shift, scale = self.modulation[:2]
        self.tokens_float = self.tokens.reshape(self.by_sample).astype(F32)
        self.normed_one, self.inverse_one = normalize(self.tokens_float)
        self.input_one = low(self.normed_one * (1.0 + scale) + shift).reshape(self.flat)

    def gather_small(self):
        self.gathered_small = self.to_all(self.small)
        self.all_activated = self.plan.gather_groups(self.activated)

    def prepare(self):
        small, heads = self.gathered_small, self.heads
        cut_one = 2 * self.local_width
        cut_two = cut_one + self.table_rows * self.local_heads
        biases = small[:, :cut_one].reshape(self.shards, 2, self.local_heads, HS).transpose(0, 2, 1, 3)
        biases = biases.reshape(heads, 2, HS).astype(F32)
        self.head_bias = self.plan.to_own(jnp.concatenate([biases, jnp.zeros_like(biases)], axis=2))
        self.entries = window_entries(self.offset_index)
        table = small[:, cut_one:cut_two].reshape(heads, self.table_rows)
        table = self.plan.to_own(table).reshape(heads, self.table_rows)
        windows = table_windows(table, self.entries)
        self.windows = windows.reshape((2, heads // 2) + windows.shape[1:])
        self.up_biases = small[:, cut_two:].astype(F32)[:, :, None]

    def forward_weights(self, number, own, other):
        self.attn_w[number] = (own, other)

    def forward(self, number):
        self.saved[number], branch = attention_forward(
            self.half,
            self.input_one,
            self.attn_w[number],
            [self.plan.chunk(number, part) for part in self.head_bias],
            [self.plan.chunk(number, part) for part in self.windows],
            self.patches,
        )
        self.branch = self.branch + [branch]

    def norm_two(self):
        _, _, gate_one, shift, scale, gate_two = self.modulation
        first = lax.axis_index("mp") * self.samples
        live = first + jnp.arange(self.samples, dtype=jnp.int32) < self.counts[0]
        self.live = live.astype(F32)[:, None, None]
        self.attn_branch = sum(self.branch).reshape(self.by_sample) + self.out_bias.astype(F32)
        self.mid = self.tokens_float + gate_one * self.attn_branch
        self.normed_two, self.inverse_two = normalize(self.mid)
        self.input_two = low(self.normed_two * (1.0 + scale) + shift).reshape(self.flat)
        self.grad_final = self.out_grad.reshape(self.by_sample).astype(F32) * self.live
        self.mlp_grad = low(gate_two * self.grad_final).reshape(self.flat)

    def units_forward(self):
        quarter = self.local_units // 4
        weights = (self.shards, 4, quarter, self.width)
        values = (self.shards, 4, quarter, self.rows)
        self.up_w = self.up_w.reshape(weights)
        self.hidden, self.slope, self.down_grad = units_call(
            units_forward_kernel,
            (),
            self.shards,
            [
                (whole, self.input_two),
                (whole, self.mlp_grad),
                (by_slot, self.up_w),
                (by_slot, self.up_biases),
            ],
            [(by_slot, values, BF16), (by_slot, values, BF16), (by_slot, weights, BF16)],
        )
        self.units_in = (self.input_two, self.mlp_grad)

    def part_order(self, part):
        shards, quarters = self.order
        slots = self.shards // 2
        return slots, (jnp.concatenate([shards[part * slots : (part + 1) * slots], quarters]),)

    def units_backward(self, part):
        slots, order = self.part_order(part)
        piece = (slots, 2, self.local_units // 4, self.width)
        own, other, sums, grad = units_call(
            units_backward_kernel,
            order,
            slots,
            [
                (whole, self.units_in[0]),
                (whole, self.units_in[1]),
                (by_shard, self.up_w),
                (by_shard, self.slope),
                (by_slot, self.down_w[part][0]),
                (by_slot, self.down_w[part][1]),
            ],
            [
                (by_slot, piece, BF16),
                (by_slot, piece, BF16),
                (by_slot, (slots, self.local_units, 1), F32),
                (whole, self.flat, F32),
            ],
        )
        self.up_grads = self.up_grads + [(own, other)]
        self.unit_sums = self.unit_sums + [sums]
        self.grad_input_two_parts = self.grad_input_two_parts + [grad]

    def norm_two_back(self):
        _, _, gate_one, _, scale, _ = self.modulation
        self.grad_input_two = sum(self.grad_input_two_parts).reshape(self.by_sample)
        grad_normed = self.grad_input_two * (1.0 + scale)
        self.grad_mid = self.grad_final + norm_back(grad_normed, self.normed_two, self.inverse_two)
        self.attn_grad = low(gate_one * self.grad_mid).reshape(self.flat)

    def backward(self, number):
        sides, rows_grad = attention_backward(
            self.half,
            self.input_one,
            self.attn_grad,
            self.attn_w[number],
            self.saved[number],
            self.windows.shape[2:],
            self.patches,
        )
        self.head_grads = {**self.head_grads, number: tuple(side[0] for side in sides)}
        self.head_extras[number] = [side[1:] for side in sides]
        self.rows_grads = self.rows_grads + [rows_grad]

    def units_out(self):
        self.mlp_parts = []
        for part in (0, 1):
            slots, order = self.part_order(part)
            self.mlp_parts += units_call(
                units_out_kernel,
                order,
                slots,
                [
                    (by_shard, self.hidden),
                    (by_slot, self.down_w[part][0]),
                    (by_slot, self.down_w[part][1]),
                ],
                [(whole, self.flat, F32)],
            )

    def finish_rows(self):
        _, scale_one, _, _, _, gate_two = self.modulation
        mlp_branch = sum(self.mlp_parts).reshape(self.by_sample) + self.down_bias.astype(F32)
        self.block_out = low((self.mid + gate_two * mlp_branch) * self.live).reshape(self.flat)
        grad_input_one = sum(self.rows_grads).reshape(self.by_sample)
        grad_normed = grad_input_one * (1.0 + scale_one)
        tokens_grad = self.grad_mid + norm_back(grad_normed, self.normed_one, self.inverse_one)
        self.tokens_grad = tokens_grad.reshape(self.flat)
        terms = (
            grad_input_one,
            grad_input_one * self.normed_one,
            self.grad_mid * self.attn_branch,
            self.grad_input_two,
            self.grad_input_two * self.normed_two,
            self.grad_final * mlp_branch,
        )
        mod_grad = low(jnp.stack([jnp.sum(term, axis=1) for term in terms], axis=1))
        mod_grad = mod_grad.reshape(self.samples, self.shards, self.columns)
        self.mod_grad = mod_grad.transpose(1, 0, 2)
        self.sums = jnp.stack(
            [jnp.sum(part.astype(F32), axis=0) for part in (self.attn_grad, self.mlp_grad)]
        )

    def extras(self, place):
        numbers = range(len(self.head_extras))
        sides = [[self.head_extras[number][side][place] for number in numbers] for side in (0, 1)]
        return self.plan.to_whole(jnp.stack([self.plan.in_slots(side) for side in sides]))

    def finish_small(self):
        shards, columns = self.shards, self.columns
        head_grads = self.extras(0)[:, :, :HS].reshape(shards, -1)
        table_grads = table_from_windows(self.extras(1), self.entries, self.table_rows).reshape(shards, -1)
        unit_grads = self.plan.units_to_whole(jnp.concatenate(self.unit_sums)).reshape(shards, -1)
        parts = [head_grads, table_grads, unit_grads, self.sums.reshape(shards, -1)]
        sizes = [part.shape[1] for part in parts]
        parts.append(self.mod_grad.reshape(shards, -1).astype(F32))
        came = self.exchange(jnp.concatenate(parts, axis=1))
        total_size = sum(sizes)
        mod_grad = low(came[:, total_size:]).reshape(self.group_samples, columns)
        act_grad = low(dot_nt(mod_grad, self.modulator)).reshape(shards, self.samples, self.width)
        act_grad = jnp.sum(self.exchange(act_grad).astype(F32), axis=0)
        totals = jnp.sum(came[:, :total_size], axis=0)
        totals = self.plan.sum_groups(totals)
        all_mod_grad = self.plan.gather_groups(mod_grad)
        self.modulator_grad = dot_tn(self.all_activated, all_mod_grad)
        self.modulator_bias_grad = jnp.sum(all_mod_grad.astype(F32), axis=0)
        cuts = [sum(sizes[:number]) for number in (1, 2, 3)]
        head_part, table_part, self.up_bias_grad, row_part = jnp.split(totals, cuts)
        head_part = head_part.reshape(self.local_heads, 2, HS).transpose(1, 0, 2)
        self.qv_bias_grad = head_part.reshape(2, self.local_width)
        self.offset_table_grad = table_part.reshape(self.local_heads, self.table_rows).T
        last = self.to_all(jnp.concatenate([act_grad.reshape(-1), row_part]))
        cut = act_grad.size
        act_grad = low(last[:, :cut]).astype(F32).reshape(self.group_samples, self.width)
        self.out_bias_grad, self.down_bias_grad = last[:, cut:].reshape(2, self.width)
        _, silu_back = jax.vjp(jax.nn.silu, self.conditioning)
        self.cond_grad = silu_back(act_grad)[0]

    def outputs(self):
        attn = self.attn_shard.reshape(self.local_heads, 4, HS, self.width)
        qkv_grad = attn[:, :3].transpose(3, 1, 0, 2).reshape(self.width, 3, self.local_width)
        return (
            self.block_out,
            self.tokens_grad,
            self.cond_grad,
            self.modulator_grad,
            self.modulator_bias_grad,
            qkv_grad,
            self.qv_bias_grad,
            self.offset_table_grad,
            attn[:, 3].reshape(self.local_width, self.width),
            self.out_bias_grad,
            self.up_shard.T,
            self.up_bias_grad,
            self.down_shard,
            self.down_bias_grad,
        )


def local(plan, *arguments):
    work = Work(plan, *arguments)
    plan.run(work)
    return work.outputs()


def solution(mesh):
    known = (mesh.shape["dp"], mesh.shape["mp"]) == (4, 8)
    plan = PairPlan(mesh) if known else PlainPlan(mesh)
    in_specs = (
        P(("dp", "mp"), None),
        P("dp", None),
        P("dp"),
        P(),
        P(None, "mp"),
        P("mp"),
        P(None, None, "mp"),
        P(None, "mp"),
        P(None, "mp"),
        P("mp", None),
        P(),
        P(None, "mp"),
        P("mp"),
        P("mp", None),
        P(),
        P(("dp", "mp"), None),
    )
    out_specs = (
        P(("dp", "mp"), None),
        P(("dp", "mp"), None),
        P("dp", None),
        P(None, "mp"),
        P("mp"),
        P(None, None, "mp"),
        P(None, "mp"),
        P(None, "mp"),
        P("mp", None),
        P(),
        P(None, "mp"),
        P("mp"),
        P("mp", None),
        P(),
    )
    return jax.shard_map(
        partial(local, plan), mesh=mesh, in_specs=in_specs, out_specs=out_specs, check_vma=False
    )
```

time: 914 us -> 608 us (0.67)
  waiting for transfers between devices: 334 us -> 98.1 us
  matrix products: 104 us -> 4.64 us
  blocking collectives: 94.6 us -> 0 us
  Pallas kernels: 99.1 us -> 178 us
  other arithmetic: 50.8 us -> 124 us
  local copies, waits for them, and re-layouts: 113 us -> 88.9 us
    ppermute x76 -> x60, waiting for transfers between devices: 271 us -> 80.5 us  [the longest x54 75.3 us: __call__(): moved = [lax.ppermute(value, BOTH, way) for value, way in moves]]
    pallas_call x0 -> x7, Pallas kernels: none -> 87.1 us  [units_call(): pl.pallas_call(kernel, grid_spec=pltpu.PrefetchScalarGridSpec(num_scalar_...]
    psum x1 -> x0, waiting for transfers between devices: 63.1 us -> none  [local(): lax.psum(jnp.concatenate([head_grads.reshape(-1), table_grads.reshape(-1)...]
    unnamed x1 -> x0, blocking collectives: 45.4 us -> none
    dot_general x9 -> x1, matrix products: 40.1 us -> 0.63 us  [modulate(): part = jnp.dot(self.activated, self.modulator, preferred_element_type=F32)]
    psum x1 -> x0, blocking collectives: 38 us -> none  [local(): act_grad = lax.psum(low(dot_nt(mod_grad, modulator)), 'mp').astype(F32)]
    dot_general x5 -> x1, matrix products: 32.7 us -> 0.37 us  [dot_nt(): lax.dot_general(left, right, (((1,), (1,)), ((), ())), preferred_element_...]
    another operation x14 -> x49, other arithmetic: 1.62 us -> 31.4 us  [the longest x22 23.9 us: run(): stack = lambda *values: jnp.stack(values)]
  transfers between devices with their start and end apart: 79 -> 68, of which waited for: 38 -> 15; matrix products, arithmetic and copies ran while one was open for 20% -> 28% of each run, Pallas kernels for 4% -> 24%
where the time goes in v2:
time: 608 us; the launch traced here: 598 us
  Pallas kernels  178 us (29%)
  other arithmetic  124 us (20%)
  waiting for transfers between devices  98.1 us (16%)
  local copies, waits for them, and re-layouts  88.9 us (15%)
  starting transfers between devices  87.2 us (14%)
  between operations  17.7 us (3%)
    pallas_call x7, Pallas kernels, units_call(): pl.pallas_call(kernel, grid_spec=pltpu.PrefetchScalarGridSpec(num_scalar_...  87.1 us
    ppermute x54, waiting for transfers between devices, __call__(): moved = [lax.ppermute(value, BOTH, way) for value, way in moves]  75.3 us
    ppermute x54, starting transfers between devices, __call__(): moved = [lax.ppermute(value, BOTH, way) for value, way in moves]  64 us
    pallas_call x4, Pallas kernels, attention_backward(): pl.pallas_call(backward_kernel, grid_spec=pltpu.PrefetchScalarGridSpec(nu...  61.5 us
    convert_element_type x24, other arithmetic, low(): return value.astype(BF16)  45.5 us
    unnamed x387, local copies, waits for them, and re-layouts  34.2 us
    pallas_call x4, Pallas kernels, attention_forward(): pl.pallas_call(forward_kernel, grid_spec=pltpu.PrefetchScalarGridSpec(num...  29 us
    another operation x22, other arithmetic, run(): stack = lambda *values: jnp.stack(values)  23.9 us
  transfers between devices with their start and end apart: 68, of which 15 were waited for; matrix products, arithmetic and copies ran while one was open for 28% of the time, Pallas kernels for 24%

profile of v2, /device:TPU:0, one launch (start us, length us, event | category | flops | bytes accessed | tf_op | source)
XLA Modules:
  0.0 598.4 jit_solution(9776764375732562404)
XLA Ops:
  56.4 9.0 %all-to-all-done.1 = bf16[8,2,1393]{2,1,0:T(2,128)(2,1)S(1)} async-done(((bf16[8,2,1393]{2,1,0:T(2,128)(2,1)}), bf16[8,2,1393]{2,1,0:T(2,128)(2,1)S(1)}, u32[]{:S(2)}, u32[]{:S(2)}) %all-to-all-start.1) | async-done | bytes 44608 | tf_op jit(solution)/shard_map/all_to_all | solution.py:796
  97.3 12.8 %collective-permute-done.10 = bf16[2,144,1152]{2,1,0:T(8,128)(2,1)S(1)} collective-permute-done((bf16[2,144,1152]{2,1,0:T(8,128)(2,1)S(1)}, bf16[2,144,1152]{2,1,0:T(8,128)(2,1)S(1)}, u32[]{:S(2)}, u32[]{:S(2)}) %collective-permute-start.10) | collective-permute-done | bytes 663584 | tf_op jit(solution)/shard_map/ppermute | solution.py:39
  119.6 8.0 %shard_map.264 = (bf16[2,512,144]{2,1,0:T(8,128)(2,1)S(1)}, bf16[2,512,144]{2,1,0:T(8,128)(2,1)S(1)}, bf16[2,2,256,256]{3,2,1,0:T(8,128)(2,1)S(1)}, bf16[2,512,1...) custom-call(s32[1]{0:T(128)} %bitcast.49.half, ...), custom_call_target="tpu_custom_call" | custom-call | flops 4378853376 | bytes 12582912 | tf_op jit(solution)/shard_map/pallas_call | solution.py:560
  135.0 6.9 %shard_map.265 = (bf16[2,512,144]{2,1,0:T(8,128)(2,1)S(1)}, bf16[2,512,144]{2,1,0:T(8,128)(2,1)S(1)}, bf16[2,2,256,256]{3,2,1,0:T(8,128)(2,1)S(1)}, bf16[2,512,1...) custom-call(s32[1]{0:T(128)} %bitcast.49.half, ...), custom_call_target="tpu_custom_call" | custom-call | flops 4378853376 | bytes 12582912 | tf_op jit(solution)/shard_map/pallas_call | solution.py:560
  142.1 10.8 %collective-permute-done.17 = bf16[2,144,1152]{2,1,0:T(8,128)(2,1)} collective-permute-done((bf16[2,144,1152]{2,1,0:T(8,128)(2,1)S(1)}, bf16[2,144,1152]{2,1,0:T(8,128)(2,1)}, u32[]{:S(2)}, u32[]{:S(2)}) %collective-permute-start.17) | collective-permute-done | bytes 663584 | tf_op jit(solution)/shard_map/ppermute | solution.py:39
  152.9 22.7 %collective-permute-done.16 = bf16[3,144,1152]{2,1,0:T(8,128)(2,1)S(1)} collective-permute-done((bf16[3,144,1152]{2,1,0:T(8,128)(2,1)}, bf16[3,144,1152]{2,1,0:T(8,128)(2,1)S(1)}, u32[]{:S(2)}, u32[]{:S(2)}) %collective-permute-start.16) | collective-permute-done | bytes 995360 | tf_op jit(solution)/shard_map/ppermute | solution.py:39
  181.2 7.0 %shard_map.266 = (bf16[2,512,144]{2,1,0:T(8,128)(2,1)S(1)}, bf16[2,512,144]{2,1,0:T(8,128)(2,1)S(1)}, bf16[2,2,256,256]{3,2,1,0:T(8,128)(2,1)S(1)}, bf16[2,512,1...) custom-call(s32[1]{0:T(128)} %bitcast.49.half, ...), custom_call_target="tpu_custom_call" | custom-call | flops 4378853376 | bytes 12582912 | tf_op jit(solution)/shard_map/pallas_call | solution.py:560
  189.1 6.4 %collective-permute-done.20 = bf16[2,144,1152]{2,1,0:T(8,128)(2,1)S(1)} collective-permute-done((bf16[2,144,1152]{2,1,0:T(8,128)(2,1)}, bf16[2,144,1152]{2,1,0:T(8,128)(2,1)S(1)}, u32[]{:S(2)}, u32[]{:S(2)}) %collective-permute-start.20) | collective-permute-done | bytes 663584 | tf_op jit(solution)/shard_map/ppermute | solution.py:39
  201.6 7.1 %shard_map.267 = (bf16[2,512,144]{2,1,0:T(8,128)(2,1)S(1)}, bf16[2,512,144]{2,1,0:T(8,128)(2,1)S(1)}, bf16[2,2,256,256]{3,2,1,0:T(8,128)(2,1)S(1)}, bf16[2,512,1...) custom-call(s32[1]{0:T(128)} %bitcast.49.half, ...), custom_call_target="tpu_custom_call" | custom-call | flops 4378853376 | bytes 12582912 | tf_op jit(solution)/shard_map/pallas_call | solution.py:560
  226.3 6.2 %fusion.78 = (f32[512]{0:T(512)S(1)}, f32[512,1152]{1,0:T(8,128)S(1)}, f32[512,1152]{1,0:T(8,128)}) fusion(f32[1152]{0:T(1024)S(1)} %convert_element_type.1237, f32[2,1152]{1,0:T(2,128)S(1)} %bitcast.487, bf16[512,1152]{1,0:T(8,128)(2,1)} %param.16, f32[512,1152]{1,0:T(8,128)} %copy-done.14, f32[512,1152]{1,0:T(8,128)} %copy-done.12, ...), kind=kLoop, calls=%fused_computation.324 | loop fusion | flops 4718080 | bytes 15351296 | tf_op jit(solution)/shard_map/reduce_sum | solution.py:725
  235.4 21.1 %shard_map.268 = (bf16[8,4,144,512]{3,2,1,0:T(8,128)(2,1)S(1)}, bf16[8,4,144,512]{3,2,1,0:T(8,128)(2,1)}, bf16[8,4,144,1152]{3,2,1,0:T(8,128)(2,1)}) custom-call(bf16[512,1152]{1,0:T(8,128)(2,1)S(1)} %fusion.5.x_ref, bf16[512,1152]{1,0:T(8,128)(2,1)S(1)} %fusion.6.g_ref, bf16[8,4,144,1152]{3,2,1,0:T(8,128)(2,1)} %bitcast.446, f32[8,576,1]{2,1,0:T(8,128)S(1)} %copy-done.6), custom_call_target="tpu_custom_call" | custom-call | flops 3200000000 | bytes 67108864 | tf_op jit(solution)/shard_map/pallas_call | solution.py:656
  258.6 15.4 %shard_map.269 = (bf16[4,2,144,1152]{3,2,1,0:T(8,128)(2,1)S(1)}, bf16[4,2,144,1152]{3,2,1,0:T(8,128)(2,1)}, f32[4,576,1]{2,1,0:T(8,128)S(1)}, f32[512,1152]{1,0:T(8,128)S(1)}) custom-call(s32[8]{0:T(128)S(1)} %concatenate.67.order, bf16[512,1152]{1,0:T(8,128)(2,1)S(1)} %fusion.5.x_ref, bf16[512,1152]{1,0:T(8,128)(2,1)S(1)} %fusion.6.g_ref, ...), custom_call_target="tpu_custom_call" | custom-call | flops 1600000000 | bytes 33554432 | tf_op jit(solution)/shard_map/pallas_call | solution.py:656
  280.0 15.6 %shard_map.270 = (bf16[4,2,144,1152]{3,2,1,0:T(8,128)(2,1)S(1)}, bf16[4,2,144,1152]{3,2,1,0:T(8,128)(2,1)}, f32[4,576,1]{2,1,0:T(8,128)S(1)}, f32[512,1152]{1,0:T(8,128)S(1)}) custom-call(s32[8]{0:T(128)S(1)} %concatenate.72.order, bf16[512,1152]{1,0:T(8,128)(2,1)S(1)} %copy-done.5, bf16[512,1152]{1,0:T(8,128)(2,1)S(1)} %fusion.6.g_ref, ...), custom_call_target="tpu_custom_call" | custom-call | flops 1600000000 | bytes 33554432 | tf_op jit(solution)/shard_map/pallas_call | solution.py:656
  319.9 5.3 fusion.13
  335.8 15.6 %shard_map.271 = (bf16[2,2,144,1152]{3,2,1,0:T(8,128)(2,1)S(1)}, f32[2,2,144]{2,1,0:T(2,128)S(1)}, f32[2,16,512]{2,1,0:T(8,128)S(1)}, bf16[2,2,144,1152]{3,2,1,0...) custom-call(s32[1]{0:T(128)} %bitcast.49.half, ...), custom_call_target="tpu_custom_call" | custom-call | flops 10267656192 | bytes 20971520 | tf_op jit(solution)/shard_map/pallas_call | solution.py:586
  356.0 15.2 %shard_map.272 = (bf16[2,2,144,1152]{3,2,1,0:T(8,128)(2,1)S(1)}, f32[2,2,144]{2,1,0:T(2,128)S(1)}, f32[2,16,512]{2,1,0:T(8,128)S(1)}, bf16[2,2,144,1152]{3,2,1,0...) custom-call(s32[1]{0:T(128)} %bitcast.49.half, ...), custom_call_target="tpu_custom_call" | custom-call | flops 10267656192 | bytes 20971520 | tf_op jit(solution)/shard_map/pallas_call | solution.py:586
  387.2 15.6 %shard_map.273 = (bf16[2,2,144,1152]{3,2,1,0:T(8,128)(2,1)S(1)}, f32[2,2,144]{2,1,0:T(2,128)S(1)}, f32[2,16,512]{2,1,0:T(8,128)S(1)}, bf16[2,2,144,1152]{3,2,1,0...) custom-call(s32[1]{0:T(128)} %bitcast.49.half, ...), custom_call_target="tpu_custom_call" | custom-call | flops 10267656192 | bytes 20971520 | tf_op jit(solution)/shard_map/pallas_call | solution.py:586
  402.9 7.4 %collective-permute-done.35 = bf16[1,144,1152]{2,1,0:T(8,128)(2,1)} collective-permute-done((bf16[1,144,1152]{2,1,0:T(8,128)(2,1)}, bf16[1,144,1152]{2,1,0:T(8,128)(2,1)}, u32[]{:S(2)}, u32[]{:S(2)}) %collective-permute-start.35) | collective-permute-done | bytes 331808 | tf_op jit(solution)/shard_map/ppermute | solution.py:39
  411.5 15.1 %shard_map.274 = (bf16[2,2,144,1152]{3,2,1,0:T(8,128)(2,1)S(1)}, f32[2,2,144]{2,1,0:T(2,128)S(1)}, f32[2,16,512]{2,1,0:T(8,128)S(1)}, bf16[2,2,144,1152]{3,2,1,0...) custom-call(s32[1]{0:T(128)} %bitcast.49.half, ...), custom_call_target="tpu_custom_call" | custom-call | flops 10267656192 | bytes 20971520 | tf_op jit(solution)/shard_map/pallas_call | solution.py:586
  442.8 15.1 %shard_map.277 = f32[16,961]{1,0:T(8,128)S(1)} custom-call(s32[16,1,512]{2,1,0:T(1,128)S(1)} %reshape.1625.entries_ref, f32[16,16,512]{2,1,0:T(8,128)S(1)} %bitcast.444), custom_call_target="tpu_custom_call" | custom-call | flops 6400000000 | bytes 134217728 | tf_op jit(solution)/shard_map/pallas_call | solution.py:656
  465.3 8.0 %collective-permute-done.39 = bf16[1,144,1152]{2,1,0:T(8,128)(2,1)} collective-permute-done((bf16[1,144,1152]{2,1,0:T(8,128)(2,1)}, bf16[1,144,1152]{2,1,0:T(8,128)(2,1)}, u32[]{:S(2)}, u32[]{:S(2)}) %collective-permute-start.39) | collective-permute-done | bytes 331808 | tf_op jit(solution)/shard_map/ppermute | solution.py:39
  487.3 8.2 %shard_map.276 = f32[512,1152]{1,0:T(8,128)S(1)} custom-call(s32[8]{0:T(128)S(1)} %concatenate.72.order, bf16[8,4,144,512]{3,2,1,0:T(8,128)(2,1)} %copy-done.3, bf16[4,2,144,1152]{3,2,1,0:T(8,128)(2,1)} %pad_maximum_fusion.1.down_ref, bf16[4,2,144,1152]{3,2,1,0:T(8,128)(2,1)} %collective-permute-done.23.down_other_ref), custom_call_target="tpu_custom_call" | custom-call | flops 1600000000 | bytes 33554432 | tf_op jit(solution)/shard_map/pallas_call | solution.py:656
  495.6 7.7 %shard_map.275 = f32[512,1152]{1,0:T(8,128)S(1)} custom-call(s32[8]{0:T(128)S(1)} %concatenate.67.order, bf16[8,4,144,512]{3,2,1,0:T(8,128)(2,1)} %copy-done.3, bf16[4,2,144,1152]{3,2,1,0:T(8,128)(2,1)S(1)} %copy-done.2, bf16[4,2,144,1152]{3,2,1,0:T(8,128)(2,1)} %collective-permute-done.22.down_other_ref), custom_call_target="tpu_custom_call" | custom-call | flops 1600000000 | bytes 33554432 | tf_op jit(solution)/shard_map/pallas_call | solution.py:656
  558.5 5.1 collective-permute-done.52
  (766 shorter events, 313.4 us)
Async XLA Ops:
  36.4 29.8 %collective-permute-start.6 = (bf16[2,2,144,1152]{3,2,1,0:T(8,128)(2,1)S(1)}, bf16[2,2,144,1152]{3,2,1,0:T(8,128)(2,1)}, u32[]{:S(2)}, u32[]{:S(2)}) collective-permute-start(bf16[2,2,144,1152]{3,2,1,0:T(8,128)(2,1)S(1)} %pad_maximum_fusion.3.refs_0_), channel_id=1, source_target_pairs={{0,8},{1,9},{2,10},{3,11},{4,12},{5,13},{6,14},{7,15},{8,0},{9,1},... | collective-permute-start | bytes 3981320 | tf_op jit(solution)/shard_map/ppermute | solution.py:39
  37.7 28.5 %collective-permute-start.7 = (bf16[2,144,1152]{2,1,0:T(8,128)(2,1)}, bf16[2,144,1152]{2,1,0:T(8,128)(2,1)}, u32[]{:S(2)}, u32[]{:S(2)}) collective-permute-start(bf16[2,144,1152]{2,1,0:T(8,128)(2,1)} %reverse_select_fusion.4), channel_id=1, source_target_pairs={{0,2},{1,3},{2,4},{3,5},{4,6},{5,7},{6,0},{7,1},{8,10},{9,11},{10,... | collective-permute-start | bytes 1990664 | tf_op jit(solution)/shard_map/ppermute | solution.py:39
  39.2 27.0 %collective-permute-start.4 = (bf16[144,1152]{1,0:T(8,128)(2,1)}, bf16[144,1152]{1,0:T(8,128)(2,1)}, u32[]{:S(2)}, u32[]{:S(2)}) collective-permute-start(bf16[144,1152]{1,0:T(8,128)(2,1)} %collective-permute-done), channel_id=1, source_target_pairs={{0,16},{1,17},{2,18},{3,19},{4,20},{5,21},{6,22},{7,23},{8,24},{9,... | collective-permute-start | bytes 995336 | tf_op jit(solution)/shard_map/ppermute | solution.py:39
  40.7 25.5 %collective-permute-start.3 = (bf16[144,1152]{1,0:T(8,128)(2,1)}, bf16[144,1152]{1,0:T(8,128)(2,1)}, u32[]{:S(2)}, u32[]{:S(2)}) collective-permute-start(bf16[144,1152]{1,0:T(8,128)(2,1)} %collective-permute-done), channel_id=1, source_target_pairs={{0,2},{1,3},{2,4},{3,5},{4,6},{5,7},{6,0},{7,1},{8,10},{9,11},{10,... | collective-permute-start | bytes 995336 | tf_op jit(solution)/shard_map/ppermute | solution.py:39
  49.7 166.2 %all-gather.3.cloned.1.call-start = ((), (), s32[]{:S(2)}) async-start(), calls=%async_computation.6 | async-start | bytes 10948608 | tf_op jit(solution)/shard_map/all_gather | solution.py:184
  66.2 407.1 %reduce-scatter.2.cloned.1.call-start = ((), (), s32[]{:S(2)}) async-start(), calls=%async_computation.7 | async-start | bytes 10948608 | tf_op jit(solution)/shard_map/reduce_scatter | solution.py:221
  66.3 31.0 %collective-permute-start.12 = (bf16[2,144,1152]{2,1,0:T(8,128)(2,1)}, bf16[2,144,1152]{2,1,0:T(8,128)(2,1)}, u32[]{:S(2)}, u32[]{:S(2)}) collective-permute-start(bf16[2,144,1152]{2,1,0:T(8,128)(2,1)} %reverse_select_fusion.4), channel_id=1, source_target_pairs={{0,6},{1,7},{2,0},{3,1},{4,2},{5,3},{6,4},{7,5},{8,14},{9,15},{10,... | collective-permute-start | bytes 1990664 | tf_op jit(solution)/shard_map/ppermute | solution.py:39
  85.4 43.8 %collective-permute-start.9 = (bf16[144,1152]{1,0:T(8,128)(2,1)}, bf16[144,1152]{1,0:T(8,128)(2,1)}, u32[]{:S(2)}, u32[]{:S(2)}) collective-permute-start(bf16[144,1152]{1,0:T(8,128)(2,1)} %get-tuple-element.467), channel_id=1, source_target_pairs={{0,2},{1,3},{2,4},{3,5},{4,6},{5,7},{6,0},{7,1},{8,10},{9,11},{10,... | collective-permute-start | bytes 995336 | tf_op jit(solution)/shard_map/ppermute | solution.py:39
  91.6 38.3 %collective-permute-start.8 = (bf16[2,144,1152]{2,1,0:T(8,128)(2,1)S(1)}, bf16[2,144,1152]{2,1,0:T(8,128)(2,1)S(1)}, u32[]{:S(2)}, u32[]{:S(2)}) collective-permute-start(bf16[2,144,1152]{2,1,0:T(8,128)(2,1)S(1)} %pad_maximum_fusion.11), channel_id=1, source_target_pairs={{0,1},{1,0},{2,3},{3,2},{4,5},{5,4},{6,7},{7,6},{8,9},{9,8},{10,11... | collective-permute-start | bytes 1990664 | tf_op jit(solution)/shard_map/ppermute | solution.py:39
  133.4 42.2 %collective-permute-start.16 = (bf16[3,144,1152]{2,1,0:T(8,128)(2,1)}, bf16[3,144,1152]{2,1,0:T(8,128)(2,1)S(1)}, u32[]{:S(2)}, u32[]{:S(2)}) collective-permute-start(bf16[3,144,1152]{2,1,0:T(8,128)(2,1)} %pad_maximum_fusion.9), channel_id=1, source_target_pairs={{0,16},{1,17},{2,18},{3,19},{4,20},{5,21},{6,22},{7,23},{8,24},{9,... | collective-permute-start | bytes 2985992 | tf_op jit(solution)/shard_map/ppermute | solution.py:39
  299.5 31.7 %collective-permute-start.28 = (bf16[4,2,144,1152]{3,2,1,0:T(8,128)(2,1)}, bf16[4,2,144,1152]{3,2,1,0:T(8,128)(2,1)}, u32[]{:S(2)}, u32[]{:S(2)}) collective-permute-start(bf16[4,2,144,1152]{3,2,1,0:T(8,128)(2,1)} %get-tuple-element.287), channel_id=1, source_target_pairs={{0,8},{1,9},{2,10},{3,11},{4,12},{5,13},{6,14},{7,15},{8,0},{9,1},... | collective-permute-start | bytes 7962632 | tf_op jit(solution)/shard_map/ppermute | solution.py:39
  301.3 273.9 %collective-permute-start.54 = (bf16[2,16,1152]{2,1,0:T(8,128)(2,1)}, bf16[2,16,1152]{2,1,0:T(8,128)(2,1)}, u32[]{:S(2)}, u32[]{:S(2)}) collective-permute-start(bf16[2,16,1152]{2,1,0:T(8,128)(2,1)} %maximum_select_fusion.4), channel_id=1, source_target_pairs={{0,16},{1,17},{2,18},{3,19},{4,20},{5,21},{6,22},{7,23},{8,24},{9,... | collective-permute-start | bytes 221192 | tf_op jit(solution)/shard_map/ppermute | solution.py:161
  310.8 236.2 %all-gather.5.cloned.1.call-start = ((), (), s32[]{:S(2)}) async-start(), calls=%async_computation.8 | async-start | bytes 1658880 | tf_op jit(solution)/shard_map/all_gather | solution.py:355
  351.5 24.6 %collective-permute-start.34 = (bf16[2,2,144,1152]{3,2,1,0:T(8,128)(2,1)S(1)}, bf16[2,2,144,1152]{3,2,1,0:T(8,128)(2,1)S(1)}, u32[]{:S(2)}, u32[]{:S(2)}) collective-permute-start(bf16[2,2,144,1152]{3,2,1,0:T(8,128)(2,1)S(1)} %get-tuple-element.305), channel_id=1, source_target_pairs={{0,8},{1,9},{2,10},{3,11},{4,12},{5,13},{6,14},{7,15},{8,0},{9,1},... | collective-permute-start | bytes 3981320 | tf_op jit(solution)/shard_map/ppermute | solution.py:39
  380.9 29.4 %collective-permute-start.35 = (bf16[1,144,1152]{2,1,0:T(8,128)(2,1)}, bf16[1,144,1152]{2,1,0:T(8,128)(2,1)}, u32[]{:S(2)}, u32[]{:S(2)}) collective-permute-start(bf16[1,144,1152]{2,1,0:T(8,128)(2,1)} %get-tuple-element.432), channel_id=1, source_target_pairs={{0,6},{1,7},{2,0},{3,1},{4,2},{5,3},{6,4},{7,5},{8,14},{9,15},{10,... | collective-permute-start | bytes 995336 | tf_op jit(solution)/shard_map/ppermute | solution.py:39
  383.6 26.7 %collective-permute-start.38 = (bf16[2,2,144,1152]{3,2,1,0:T(8,128)(2,1)S(1)}, bf16[2,2,144,1152]{3,2,1,0:T(8,128)(2,1)S(1)}, u32[]{:S(2)}, u32[]{:S(2)}) collective-permute-start(bf16[2,2,144,1152]{3,2,1,0:T(8,128)(2,1)S(1)} %get-tuple-element.319), channel_id=1, source_target_pairs={{0,8},{1,9},{2,10},{3,11},{4,12},{5,13},{6,14},{7,15},{8,0},{9,1},... | collective-permute-start | bytes 3981320 | tf_op jit(solution)/shard_map/ppermute | solution.py:39
  384.8 25.6 %collective-permute-start.37 = (bf16[2,144,1152]{2,1,0:T(8,128)(2,1)}, bf16[2,144,1152]{2,1,0:T(8,128)(2,1)}, u32[]{:S(2)}, u32[]{:S(2)}) collective-permute-start(bf16[2,144,1152]{2,1,0:T(8,128)(2,1)} %pad_maximum_fusion.19), channel_id=1, source_target_pairs={{0,16},{1,17},{2,18},{3,19},{4,20},{5,21},{6,22},{7,23},{8,24},{9,... | collective-permute-start | bytes 1990664 | tf_op jit(solution)/shard_map/ppermute | solution.py:39
  438.6 26.6 %collective-permute-start.40 = (bf16[1,144,1152]{2,1,0:T(8,128)(2,1)}, bf16[1,144,1152]{2,1,0:T(8,128)(2,1)}, u32[]{:S(2)}, u32[]{:S(2)}) collective-permute-start(bf16[1,144,1152]{2,1,0:T(8,128)(2,1)} %fusion.35), channel_id=1, source_target_pairs={{0,1},{1,0},{2,3},{3,2},{4,5},{5,4},{6,7},{7,6},{8,9},{9,8},{10,11... | collective-permute-start | bytes 995336 | tf_op jit(solution)/shard_map/ppermute | solution.py:39
  441.5 31.8 %collective-permute-start.41 = (bf16[2,144,1152]{2,1,0:T(8,128)(2,1)}, bf16[2,144,1152]{2,1,0:T(8,128)(2,1)}, u32[]{:S(2)}, u32[]{:S(2)}) collective-permute-start(bf16[2,144,1152]{2,1,0:T(8,128)(2,1)} %pad_maximum_fusion.20), channel_id=1, source_target_pairs={{0,16},{1,17},{2,18},{3,19},{4,20},{5,21},{6,22},{7,23},{8,24},{9,... | collective-permute-start | bytes 1990664 | tf_op jit(solution)/shard_map/ppermute | solution.py:39
  442.8 30.5 %collective-permute-start.42 = (bf16[2,2,144,1152]{3,2,1,0:T(8,128)(2,1)}, bf16[2,2,144,1152]{3,2,1,0:T(8,128)(2,1)}, u32[]{:S(2)}, u32[]{:S(2)}) collective-permute-start(bf16[2,2,144,1152]{3,2,1,0:T(8,128)(2,1)} %get-tuple-element.334), channel_id=1, source_target_pairs={{0,8},{1,9},{2,10},{3,11},{4,12},{5,13},{6,14},{7,15},{8,0},{9,1},... | collective-permute-start | bytes 3981320 | tf_op jit(solution)/shard_map/ppermute | solution.py:39
  478.1 26.1 %collective-permute-start.45 = (bf16[1,144,1152]{2,1,0:T(8,128)(2,1)}, bf16[1,144,1152]{2,1,0:T(8,128)(2,1)}, u32[]{:S(2)}, u32[]{:S(2)}) collective-permute-start(bf16[1,144,1152]{2,1,0:T(8,128)(2,1)} %fusion.32), channel_id=1, source_target_pairs={{0,6},{1,7},{2,0},{3,1},{4,2},{5,3},{6,4},{7,5},{8,14},{9,15},{10,... | collective-permute-start | bytes 995336 | tf_op jit(solution)/shard_map/ppermute | solution.py:39
  504.2 25.0 %collective-permute-start.48 = (bf16[2,144,1152]{2,1,0:T(8,128)(2,1)}, bf16[2,144,1152]{2,1,0:T(8,128)(2,1)}, u32[]{:S(2)}, u32[]{:S(2)}) collective-permute-start(bf16[2,144,1152]{2,1,0:T(8,128)(2,1)} %pad_maximum_fusion.24), channel_id=1, source_target_pairs={{0,16},{1,17},{2,18},{3,19},{4,20},{5,21},{6,22},{7,23},{8,24},{9,... | collective-permute-start | bytes 1990664 | tf_op jit(solution)/shard_map/ppermute | solution.py:39
  546.3 36.3 %collective-permute-start.57 = (bf16[2,144,1152]{2,1,0:T(8,128)(2,1)S(1)}, bf16[2,144,1152]{2,1,0:T(8,128)(2,1)}, u32[]{:S(2)}, u32[]{:S(2)}) collective-permute-start(bf16[2,144,1152]{2,1,0:T(8,128)(2,1)S(1)} %pad_maximum_fusion.25), channel_id=1, source_target_pairs={{0,16},{1,17},{2,18},{3,19},{4,20},{5,21},{6,22},{7,23},{8,24},{9,... | collective-permute-start | bytes 1990664 | tf_op jit(solution)/shard_map/ppermute | solution.py:39
  547.0 35.6 %collective-permute-start.58 = (bf16[2,144,1152]{2,1,0:T(8,128)(2,1)S(1)}, bf16[2,144,1152]{2,1,0:T(8,128)(2,1)}, u32[]{:S(2)}, u32[]{:S(2)}) collective-permute-start(bf16[2,144,1152]{2,1,0:T(8,128)(2,1)S(1)} %add_convert_fusion.1), channel_id=1, source_target_pairs={{0,8},{1,9},{2,10},{3,11},{4,12},{5,13},{6,14},{7,15},{8,0},{9,1},... | collective-permute-start | bytes 1990664 | tf_op jit(solution)/shard_map/ppermute | solution.py:39
  (219 other events, 2643.8 us)
Sparse Core Ops, SparseCore 0:
  66.4 122.6 all-gather.2
  311.0 158.0 reduce-scatter.1
  478.2 25.3 all-gather.4
